TPU v7x, 512 devices: a whole 4x4x16 slice. The times are simulated.
512 devices in a mesh: seqa: 16 (over z_lo, core), seqb: 32 (over y, z_hi, x).
Axes of the slice: x: 4, y: 4, z: 16 (z_hi: 2, z_lo: 8; z = z_hi * 8 + z_lo), core: 2. Of those that a mesh axis runs over, the one named last changes fastest.
Arguments:
- sequence_input: bfloat16 [262144, 640], P(('seqa', 'seqb')), may hold values from -6 to 6
- w_prev: bfloat16 [3, 640, 1280], P(None, 'seqa'), may hold values from -0.15625 to 0.15625
- w_now: bfloat16 [3, 640, 1280], P(None, 'seqa'), may hold values from -0.15625 to 0.15625
- conv_bias: float32 [3, 1280], replicated, may hold values from -4 to 4
- w_mix: bfloat16 [3, 640, 640], P(None, None, 'seqa'), may hold values from -0.25 to 0.25
Outputs:
- seq_out: bfloat16 [262144, 640], P(('seqa', 'seqb'))
All inputs are finite; a program needn't handle non-finite values.
Results may differ from a plain program's by a relative error of at most 0.0052.
Values may be sent and summed in bfloat16 or wider, within the bound.
No kernel may reach another device: no remote copies, remote signals or barrier semaphores. Data moves between devices by JAX's collectives and lax.ppermute only.
A program may use at most 64 MiB of HBM per device.

v0:
```python
import jax
import jax.numpy as jnp
from jax import lax
from jax.sharding import Mesh
from jax.sharding import PartitionSpec as P

D = 640
DILATION_FIRST1 = 128
DILATION_SECOND2 = 512
DILATION_THIRD3 = 2048
SEQA = ("seqa_0", "seqa_1")
SEQA_SEQB = ("seqa_0", "seqa_1", "seqb")


def from_behind(value, axis, by):
    peers = lax.axis_size(axis)
    pairs = [(i, i + by) for i in range(peers) if 0 <= i + by < peers]
    return lax.ppermute(value, axis, pairs)


def in_one_piece(arrays, axis, dim, along):
    ends, at = ([], 0)
    for a in arrays[:-1]:
        at += a.shape[along]
        ends.append(at)
    both = jnp.concatenate(arrays, axis=along)
    return tuple(jnp.split(lax.all_gather(both, axis, axis=dim, tiled=True), ends, axis=along))


def in_order(blocks, dim):
    blocks = jnp.moveaxis(blocks, 0, dim)
    dims = blocks.shape
    return blocks.reshape(*dims[:dim], dims[dim] * dims[dim + 1], *dims[dim + 2 :])


def stacked_from(value, axes, sequence):
    blocks = value
    for k in sequence:
        blocks = lax.all_gather(blocks, axes[k])
    done = sequence[::-1]
    back = [done.index(k) for k in range(len(axes))]
    blocks = blocks.transpose(*back, *range(len(axes), blocks.ndim))
    return blocks.reshape(-1, *value.shape)


def gather_axes(value, axes, sequence, dim):
    return in_order(stacked_from(value, axes, sequence), dim)


def norm_rows(values):
    scale = lax.rsqrt(jnp.mean(values * values, axis=1, keepdims=True) + 1e-06)
    return (values * scale).astype(jnp.bfloat16)


def strided_prior(normed, dilation_step):
    rows = normed.shape[0]
    reach = dilation_step // lax.axis_size("seqb")
    carried = from_behind(normed[rows - reach :], SEQA, 1)
    return jnp.concatenate([carried, normed[: rows - reach]], axis=0)


def one_layer(hidden_state, tap_prev, tap_now, bias, mixing, dilation_step):
    normed = norm_rows(hidden_state)
    earlier = strided_prior(normed, dilation_step)
    rows = hidden_state.shape[0]
    start_sum = jnp.broadcast_to(bias[None, :], (rows, bias.shape[0]))
    total = start_sum
    pieces = in_one_piece((tap_prev, tap_now), SEQA, 0, 1)
    total = total + jnp.dot(earlier, pieces[0], preferred_element_type=jnp.float32)
    pre = total + jnp.dot(normed, pieces[1], preferred_element_type=jnp.float32)
    hidden = (pre[:, :D] * jax.nn.sigmoid(pre[:, D:])).astype(jnp.bfloat16)
    return hidden_state + jnp.dot(
        hidden, gather_axes(mixing, SEQA, (0, 1), 1), preferred_element_type=jnp.float32
    )


def local(sequence_input, w_prev, w_now, conv_bias, w_mix):
    lanes = lax.axis_size("seqb")
    rows = sequence_input.shape[0]
    folded = sequence_input.reshape(rows // lanes, lanes, D)
    moved = lax.all_to_all(folded, "seqb", split_axis=1, concat_axis=0, tiled=True)
    hidden_state = moved.reshape(rows, D).astype(jnp.float32)
    for layer_index, dilation_step in enumerate(
        (DILATION_FIRST1, DILATION_SECOND2, DILATION_THIRD3)
    ):
        hidden_state = one_layer(
            hidden_state,
            w_prev[layer_index],
            w_now[layer_index],
            conv_bias[layer_index],
            w_mix[layer_index],
            dilation_step,
        )
    block_output = hidden_state.astype(jnp.bfloat16)
    back = lax.all_to_all(
        block_output.reshape(rows, 1, D), "seqb", split_axis=0, concat_axis=1, tiled=True
    )
    block_output = back.reshape(rows, D)
    return block_output


def solution(mesh):
    finer = Mesh(mesh.devices.reshape(8, 2, mesh.shape["seqb"]), ("seqa_0", "seqa_1", "seqb"))
    in_specs = (
        P(SEQA_SEQB, None),
        P(None, SEQA, None),
        P(None, SEQA, None),
        P(),
        P(None, None, SEQA),
    )
    out_specs = P(SEQA_SEQB, None)
    return jax.shard_map(local, mesh=finer, in_specs=in_specs, out_specs=out_specs, check_vma=False)
```

profile of v0, /device:TPU:2, one launch (start us, length us, event | category | flops | bytes accessed | tf_op | source)
XLA Modules:
  0.0 395.9 jit_solution(11501816091674587328)
XLA Ops:
  6.5 1.2 slice_bitcast_fusion
  7.8 0.7 pad_maximum_fusion
  8.5 0.0 all-gather.9.cloned.1.call-start
  8.6 0.7 pad_maximum_fusion.1
  9.2 0.0 all-gather.9.cloned.1.call-update
  9.3 1.0 copy.26
  10.3 20.9 %all-to-all-start = ((bf16[16,32,640]{2,0,1:T(8,128)(2,1)}), bf16[16,32,640]{2,0,1:T(8,128)(2,1)S(1)}, u32[]{:S(2)}, u32[]{:S(2)}) async-start(bf16[16,32,640]{2,0,1:T(8,128)(2,1)} %copy.26), calls=%async_computation | async-start | bytes 1310720 | tf_op jit(solution)/shard_map/all_to_all | solution.py:81
  31.2 0.0 all-gather.11.cloned.1.call-start
  31.3 0.7 pad_maximum_fusion.2
  32.0 77.0 %all_gather.37 = bf16[8,640,40]{1,2,0:T(8,128)(2,1)S(1)} all-gather(bf16[1,640,40]{1,2,0:T(8,128)(2,1)S(1)} %get-tuple-element.15), channel_id=1, replica_groups=mesh['seqa_0'=8,'seqa_1'=2,'seqb'=32] {'seqa_0'}, dimensions={0}, use_global_device_ids=true | all-gather | bytes 460800 | tf_op jit(solution)/shard_map/all_gather | solution.py:39
  109.0 2.4 all-gather
  111.4 1.0 copy.27
  112.3 47.8 %all_gather.41 = bf16[8,640,40]{1,2,0:T(8,128)(2,1)S(1)} all-gather(bf16[1,640,40]{1,2,0:T(8,128)(2,1)S(1)} %get-tuple-element.16), channel_id=1, replica_groups=mesh['seqa_0'=8,'seqa_1'=2,'seqb'=32] {'seqa_0'}, dimensions={0}, use_global_device_ids=true | all-gather | bytes 460800 | tf_op jit(solution)/shard_map/all_gather | solution.py:39
  160.1 2.4 all-gather.1
  162.5 1.0 copy.28
  163.5 48.3 %all_gather.45 = bf16[8,640,40]{1,2,0:T(8,128)(2,1)S(1)} all-gather(bf16[1,640,40]{1,2,0:T(8,128)(2,1)S(1)} %get-tuple-element.14), channel_id=1, replica_groups=mesh['seqa_0'=8,'seqa_1'=2,'seqb'=32] {'seqa_0'}, dimensions={0}, use_global_device_ids=true | all-gather | bytes 460800 | tf_op jit(solution)/shard_map/all_gather | solution.py:39
  211.8 2.5 all-gather.2
  214.3 0.1 copy.29
  214.5 0.2 multiply_reduce_fusion.2
  214.7 0.1 rsqrt.28
  214.8 0.2 fusion.25
  215.0 2.0 collective-permute-start
  217.0 0.1 convert_element_type.52
  217.1 0.0 all-gather.7.cloned.1.call-done
  217.2 2.8 fusion.9
  220.0 1.2 fusion
  221.2 1.0 multiply_reduce_fusion.1
  222.2 0.2 multiply_convert_fusion.1
  222.3 1.9 collective-permute-start.1
  224.3 16.4 %all-gather.9.cloned.1.call-done = bf16[640,2560]{1,0:T(8,128)(2,1)} async-done(((bf16[40,2560]{1,0:T(8,128)(2,1)}), bf16[640,2560]{1,0:T(8,128)(2,1)}) %all-gather.9.cloned.1.call-update) | async-done | bytes 3276816 | tf_op jit(solution)/shard_map/all_gather | solution.py:27
  240.7 2.8 fusion.6
  243.4 0.1 slice.101
  243.5 1.2 fusion.1
  244.7 1.0 multiply_reduce_fusion
  245.7 0.2 multiply_convert_fusion
  245.9 1.3 collective-permute-start.2
  247.2 99.7 %all-gather.11.cloned.1.call-done = bf16[640,2560]{1,0:T(8,128)(2,1)} async-done(((bf16[40,2560]{1,0:T(8,128)(2,1)}), bf16[640,2560]{1,0:T(8,128)(2,1)}) %all-gather.11.cloned.1.call-update) | async-done | bytes 3276816 | tf_op jit(solution)/shard_map/all_gather | solution.py:27
  346.9 2.8 fusion.3
  349.7 0.1 slice.105
  349.8 1.2 fusion.2
  351.0 0.9 fusion.29
  351.9 0.5 broadcast.84
  352.4 1.1 reduce.9
  353.5 0.1 reshape.86
  353.7 34.1 %all_to_all.24 = bf16[32,2,5120]{2,1,0:T(2,128)(2,1)S(1)} all-to-all(bf16[32,2,5120]{2,1,0:T(2,128)(2,1)S(1)} %reshape.86), channel_id=1, replica_groups=mesh['seqa_0'=8,'seqa_1'=2,'seqb'=32] {'seqb'}, dimensions={0} | all-to-all | bytes 1310720 | tf_op jit(solution)/shard_map/all_to_all | solution.py:95
  387.7 0.5 reshape.87
  388.3 0.1 copy.32
  388.4 1.0 copy.31
  (31 shorter events, 0.2 us)
Async XLA Ops:
  6.5 2.7 copy-start.5
  6.5 210.6 %all-gather.7.cloned.1.call-start = ((), (), s32[]{:S(2)}) async-start(), calls=%async_computation.2 | async-start | bytes 3481600 | tf_op jit(solution)/shard_map/all_gather | solution.py:27
  8.5 232.1 %all-gather.9.cloned.1.call-start = ((), (), s32[]{:S(2)}) async-start(), calls=%async_computation.3 | async-start | bytes 3481600 | tf_op jit(solution)/shard_map/all_gather | solution.py:27
  9.3 22.7 %copy-start.6 = (bf16[3,640,40]{1,2,0:T(8,128)(2,1)S(1)}, bf16[3,640,40]{1,2,0:T(8,128)(2,1)}, u32[]{:S(2)}) copy-start(bf16[3,640,40]{1,2,0:T(8,128)(2,1)} %param.9) | copy-start | bytes 460804
  10.3 204.1 %all-to-all-start = ((bf16[16,32,640]{2,0,1:T(8,128)(2,1)}), bf16[16,32,640]{2,0,1:T(8,128)(2,1)S(1)}, u32[]{:S(2)}, u32[]{:S(2)}) async-start(bf16[16,32,640]{2,0,1:T(8,128)(2,1)} %copy.26), calls=%async_computation | async-start | bytes 1310720 | tf_op jit(solution)/shard_map/all_to_all | solution.py:81
  31.2 315.7 %all-gather.11.cloned.1.call-start = ((), (), s32[]{:S(2)}) async-start(), calls=%async_computation.4 | async-start | bytes 3481600 | tf_op jit(solution)/shard_map/all_gather | solution.py:27
  211.8 2.6 copy-start.7
  215.0 5.0 %collective-permute-start = (bf16[4,640]{1,0:T(4,128)(2,1)S(1)}, bf16[4,640]{1,0:T(4,128)(2,1)S(1)}, u32[]{:S(2)}, u32[]{:S(2)}) collective-permute-start(bf16[4,640]{1,0:T(4,128)(2,1)S(1)} %slice.96), channel_id=1, source_target_pairs={{0,32},{32,64},{64,96},{96,128},{128,160},{160,192},{192,224},{224... | collective-permute-start | bytes 15368 | tf_op jit(solution)/shard_map/ppermute | solution.py:18
  217.2 2.8 copy-start.2
  220.0 1.2 copy-start.4
  222.3 21.1 %collective-permute-start.1 = (bf16[16,640]{1,0:T(8,128)(2,1)S(1)}, bf16[16,640]{1,0:T(8,128)(2,1)S(1)}, u32[]{:S(2)}, u32[]{:S(2)}) collective-permute-start(bf16[16,640]{1,0:T(8,128)(2,1)S(1)} %slice.100), channel_id=1, source_target_pairs={{0,32},{32,64},{64,96},{96,128},{128,160},{160,192},{192,224},{224... | collective-permute-start | bytes 61448 | tf_op jit(solution)/shard_map/ppermute | solution.py:18
  240.7 2.8 copy-start.1
  243.5 1.2 copy-start.3
  245.9 103.9 %collective-permute-start.2 = (bf16[64,640]{1,0:T(8,128)(2,1)S(1)}, bf16[64,640]{1,0:T(8,128)(2,1)S(1)}, u32[]{:S(2)}, u32[]{:S(2)}) collective-permute-start(bf16[64,640]{1,0:T(8,128)(2,1)S(1)} %slice.104), channel_id=1, source_target_pairs={{0,32},{32,64},{64,96},{96,128},{128,160},{160,192},{192,224},{224... | collective-permute-start | bytes 245768 | tf_op jit(solution)/shard_map/ppermute | solution.py:18
  346.9 2.8 copy-start
Sparse Core Ops, SparseCore 0:
  9.4 124.0 all-gather.6
  135.6 104.9 all-gather.8
  242.7 104.1 all-gather.10
where the time goes:
time: 396 us
  blocking collectives  214 us (54%)
  waiting for transfers between devices  116 us (29%)
  starting transfers between devices  26.2 us (7%)
  matrix products  14.7 us (4%)
  between operations  13.4 us (3%)
  local copies, waits for them, and re-layouts  6.86 us (2%)
  other arithmetic  3.99 us (1%)
    all_gather x6, blocking collectives, stacked_from(): blocks = lax.all_gather(blocks, axes[k])  180 us
    all_gather x3, waiting for transfers between devices, in_one_piece(): lax.all_gather(both, axis, axis=dim, tiled=True)  116 us
    all_to_all x1, blocking collectives, local(): lax.all_to_all(block_output.reshape(rows, 1, D), 'seqb', split_axis=0, co...  34.1 us
    all_to_all x1, starting transfers between devices, local(): lax.all_to_all(folded, 'seqb', split_axis=1, concat_axis=0, tiled=True)  20.9 us
    dot_general x3, matrix products, one_layer(): pre = total + jnp.dot(normed, pieces[1], preferred_element_type=jnp.float32)  8.32 us
  transfers between devices with their start and end apart: 7, of which 2 were waited for; matrix products, arithmetic and copies ran while one was open for 5% of the time, Pallas kernels for 0%

commit v1 on v0

v1 whole, which is shorter than its diff:
```python
import jax
import jax.numpy as jnp
from jax import lax
from jax.experimental import pallas as pl
from jax.experimental.pallas import tpu as pltpu
from jax.sharding import Mesh
from jax.sharding import PartitionSpec as P

D = 640
BLOCK = 512
TAIL = 128
TILE = 256
AXES = ("zl", "core", "y", "zh", "x")
SIZES = (8, 2, 4, 2, 4)
DEVICES = 512
Z_SLOTS = (-1, 0, 1, 2, 3, 4, -3, -2)


def index_of(z, core, y, x):
    z, y, x = z % 16, y % 4, x % 4
    return (((z % 8) * 2 + core) * 4 + y) * 8 + (z // 8) * 4 + x


def permuted(value, target):
    pairs = []
    for z in range(16):
        for core in range(2):
            for y in range(4):
                for x in range(4):
                    pairs.append((index_of(z, core, y, x), index_of(*target(z, core, y, x))))
    return lax.ppermute(value, AXES, pairs)


def shifted(value, target):
    pairs = [(b, target(b)) for b in range(DEVICES)]
    return lax.ppermute(value, AXES, [(a, b) for a, b in pairs if b < DEVICES])


def from_z(value, by):
    return permuted(value, lambda z, core, y, x: (z - by, core, y, x))


def from_first(value, by):
    return permuted(
        value, lambda z, core, y, x: (z, core, y, x - by) if core == 0 else (z, core, y - by, x)
    )


def from_second(value, by):
    return permuted(
        value, lambda z, core, y, x: (z, core, y - by, x) if core == 0 else (z, core, y, x - by)
    )


def from_sibling(value):
    return permuted(value, lambda z, core, y, x: (z, 1 - core, y, x))


def normed(values):
    scale = lax.rsqrt(jnp.mean(values * values, axis=1, keepdims=True) + 1e-06)
    return (values * scale).astype(jnp.bfloat16)


def kernel(
    where, s_ref, a_ref, r_ref, b_ref, ts_ref, tr_ref, perm_ref, bias_ref,
    g0, g1, g2, g3, h0, h1, h2, h3,
    out_ref, taps, mix, x0, u1, u2, x1, u3, sems,
):
    x, y, core = where[0], where[1], where[2]
    for half, arrays in enumerate(((g0, g1, g2, g3), (h0, h1, h2, h3))):
        x_first = (core + half) % 2 == 0
        for j in range(4):
            for i in range(4):
                px = (x + jnp.where(x_first, i, j)) % 4
                py = (y + jnp.where(x_first, j, i)) % 4
                rows = pl.multiple_of((px // 2) * D + half * 320, 320)
                columns = pl.multiple_of((px % 2) * D, D)
                source = arrays[j].at[i]

                @pl.when(py < 3)
                def _():
                    pltpu.make_async_copy(
                        source, taps.at[py, pl.ds(rows, 320), pl.ds(columns, D)], sems.at[py]
                    ).start()

                @pl.when((py == 3) & (px < 3))
                def _():
                    pltpu.make_async_copy(
                        source, mix.at[px, pl.ds(half * 320, 320)], sems.at[3]
                    ).start()

    def bring(ref, slot, tail_slot, start, count):
        exact = jnp.dot(ref[start : start + count], perm_ref[...], preferred_element_type=jnp.float32)
        x0[slot, start : start + count] = exact.astype(jnp.bfloat16)
        unit = normed(exact)
        u1[slot, TAIL + start : TAIL + start + count] = unit
        if tail_slot is not None and start + count == BLOCK:
            u1[tail_slot, :TAIL] = unit[count - TAIL :]

    def bring_tail(ref, slot):
        exact = jnp.dot(ref[...], perm_ref[...], preferred_element_type=jnp.float32)
        u1[slot, :TAIL] = normed(exact)

    a_slot = jnp.where(x == 0, 0, 2)
    t_slot = jnp.where(x < 2, 0, 2)
    for start in range(0, BLOCK, TILE):
        bring(s_ref, 3, None, start, TILE)
        bring(r_ref, 1, None, start, TILE)
        bring(a_ref, a_slot, a_slot + 1, start, TILE)
        bring(b_ref, 2 - a_slot, 3 - a_slot, start, TILE)
    bring_tail(ts_ref, t_slot)
    bring_tail(tr_ref, 2 - t_slot)

    def layer(prev, now, held, index):
        both = jnp.concatenate([prev, now], axis=1)
        pre = jnp.dot(both, taps[index], preferred_element_type=jnp.float32)
        pre = pre + bias_ref[index : index + 1, :]
        hidden = (pre[:, :D] * jax.nn.sigmoid(pre[:, D:])).astype(jnp.bfloat16)
        return held + lax.dot_general(
            hidden, mix[index], (((1,), (1,)), ((), ())), preferred_element_type=jnp.float32
        )

    pltpu.make_async_copy(mix, mix, sems.at[3]).wait()
    pltpu.make_async_copy(taps.at[0], taps.at[0], sems.at[0]).wait()

    @pl.loop(0, 8)
    def _(step):
        slot = step // 2
        start = pl.multiple_of((step % 2) * TILE, TILE)
        rows = pl.ds(start, TILE)
        now = u1[slot, pl.ds(pl.multiple_of(start + TAIL, TAIL), TILE)]
        after = layer(u1[slot, rows], now, x0[slot, rows].astype(jnp.float32), 0)
        unit = normed(after)
        u2[slot, rows] = jnp.where(where[3 + slot] != 0, unit, jnp.zeros_like(unit))
        x1[slot, rows] = after

    pltpu.make_async_copy(taps.at[1], taps.at[1], sems.at[1]).wait()

    @pl.loop(0, 4)
    def _(step):
        slot = (step // 2) * 2 + 1
        rows = pl.ds(pl.multiple_of((step % 2) * TILE, TILE), TILE)
        after = layer(u2[slot - 1, rows], u2[slot, rows], x1[slot, rows], 1)
        unit = normed(after)
        u3[step // 2, rows] = jnp.where(where[3 + slot] != 0, unit, jnp.zeros_like(unit))
        x1[slot, rows] = after

    pltpu.make_async_copy(taps.at[2], taps.at[2], sems.at[2]).wait()

    @pl.loop(0, 2)
    def _(step):
        rows = pl.ds(pl.multiple_of(step * TILE, TILE), TILE)
        after = layer(u3[0, rows], u3[1, rows], x1[3, rows], 2).astype(jnp.bfloat16)
        out_ref[rows, :] = lax.dot_general(
            after, perm_ref[...], (((1,), (1,)), ((), ())), preferred_element_type=jnp.float32
        ).astype(jnp.bfloat16)


def block_output(where, rows_in, perm, bias, weights):
    vmem = pl.BlockSpec(memory_space=pltpu.VMEM)
    hbm = pl.BlockSpec(memory_space=pl.ANY)
    return pl.pallas_call(
        kernel,
        out_shape=jax.ShapeDtypeStruct((BLOCK, D), jnp.bfloat16),
        in_specs=[pl.BlockSpec(memory_space=pltpu.SMEM)] + [vmem] * 8 + [hbm] * 8,
        out_specs=vmem,
        scratch_shapes=[
            pltpu.VMEM((3, 2 * D, 2 * D), jnp.bfloat16),
            pltpu.VMEM((3, D, D), jnp.bfloat16),
            pltpu.VMEM((4, BLOCK, D), jnp.bfloat16),
            pltpu.VMEM((4, TAIL + BLOCK, D), jnp.bfloat16),
            pltpu.VMEM((4, BLOCK, D), jnp.bfloat16),
            pltpu.VMEM((4, BLOCK, D), jnp.float32),
            pltpu.VMEM((2, BLOCK, D), jnp.bfloat16),
            pltpu.SemaphoreType.DMA((4,)),
        ],
        compiler_params=pltpu.CompilerParams(vmem_limit_bytes=56 * 1024 * 1024),
        cost_estimate=pl.CostEstimate(flops=15_000_000_000, bytes_accessed=16_000_000, transcendentals=3_000_000),
    )(where, *rows_in, perm, bias, *weights)


def local(sequence_input, w_prev, w_now, conv_bias, w_mix):
    zl, core, y, zh, x = (lax.axis_index(a) for a in AXES)
    block = (((zl * 2 + core) * 4 + y) * 2 + zh) * 4 + x

    at = jnp.minimum(y, 2)
    tap_prev = lax.dynamic_slice(w_prev, (at, 0, (x % 2) * D), (1, 40, D))[0]
    tap_now = lax.dynamic_slice(w_now, (at, 0, (x % 2) * D), (1, 40, D))[0]
    mixing = lax.dynamic_slice(w_mix, (jnp.minimum(x, 2), 0, 0), (1, D, 40))[0].T
    piece = jnp.where(y == 3, mixing, jnp.where(x < 2, tap_prev, tap_now))

    above, below = from_z(piece, 1), from_z(piece, -1)
    three = jnp.concatenate([below, piece, above])
    far_above, far_below = from_z(three, 3), from_z(three[40:], -3)
    whole = jnp.concatenate([three, far_above, far_below])

    own = sequence_input
    far = shifted(own, lambda b: b + 4)
    beside = shifted(own, lambda b: b + 1 if b % 4 < 3 else b + 5)
    own_tail = shifted(own[BLOCK - TAIL :], lambda b: b + 2 if b % 4 < 2 else b + 6)
    far_beside = permuted(far, lambda z, c, yy, xx: (z, c, yy, xx + 1))
    far_tail = permuted(far[BLOCK - TAIL :], lambda z, c, yy, xx: (z, c, yy, xx + 2))

    line = jnp.stack([whole] + [from_first(whole, by) for by in (1, 2, 3)])
    mine = [line] + [from_second(line, by) for by in (1, 2, 3)]
    theirs = [from_sibling(v) for v in mine]

    k = jnp.arange(D)
    slot = (k % 320) // 40
    shard = (zl + jnp.asarray(Z_SLOTS, jnp.int32)[slot]) % 8
    channel = (shard * 2 + jnp.where(k < 320, core, 1 - core)) * 40 + k % 40
    perm = (k[:, None] == channel[None, :]).astype(jnp.bfloat16)

    where = jnp.stack(
        [x, y, core, block >= 5, block >= 4, block >= 1, block >= 0, block]
    ).astype(jnp.int32)
    rows_in = (own, beside, far, far_beside, own_tail, far_tail)
    return block_output(where, rows_in, perm, conv_bias, mine + theirs)


def solution(mesh):
    finer = Mesh(mesh.devices.reshape(SIZES), AXES)
    seqa, seqb = AXES[:2], AXES[2:]
    in_specs = (P(AXES, None), P(None, seqa, None), P(None, seqa, None), P(), P(None, None, seqa))
    return jax.shard_map(
        local, mesh=finer, in_specs=in_specs, out_specs=P(AXES, None), check_vma=False
    )
```

time: 396 us -> 226 us (0.57)
  the two profiles are of different devices: /device:TPU:2 before, /device:TPU:96 now
where the time goes in v1:
time: 226 us; the launch traced here: 225 us
  waiting for transfers between devices  112 us (50%)
  starting transfers between devices  74.3 us (33%)
  Pallas kernels  35.2 us (16%)
  other arithmetic  2.41 us (1%)
    ppermute x3, waiting for transfers between devices, shifted(): return lax.ppermute(value, AXES, [(a, b) for a, b in pairs if b < DEVICES])  81.2 us
    ppermute x16, starting transfers between devices, permuted(): return lax.ppermute(value, AXES, pairs)  58.5 us
    pallas_call x1, Pallas kernels, block_output(): pl.pallas_call(kernel, out_shape=jax.ShapeDtypeStruct((BLOCK, D), jnp.bfl...  35.2 us
    ppermute x16, waiting for transfers between devices, permuted(): return lax.ppermute(value, AXES, pairs)  30.6 us
    ppermute x3, starting transfers between devices, shifted(): return lax.ppermute(value, AXES, [(a, b) for a, b in pairs if b < DEVICES])  15.8 us
  transfers between devices with their start and end apart: 19, of which 9 were waited for; matrix products, arithmetic and copies ran while one was open for 1% of the time, Pallas kernels for 0%

profile of v1, /device:TPU:96, one launch (start us, length us, event | category | flops | bytes accessed | tf_op | source)
XLA Modules:
  0.0 224.9 jit_solution(12827497522216055180)
XLA Ops:
  0.0 0.9 bitcast_select_fusion
  0.9 2.0 collective-permute-start.6
  2.9 5.0 %collective-permute-start.5 = (bf16[40,640]{1,0:T(8,128)(2,1)S(1)}, bf16[40,640]{1,0:T(8,128)(2,1)S(1)}, u32[]{:S(2)}, u32[]{:S(2)}) collective-permute-start(bf16[40,640]{1,0:T(8,128)(2,1)S(1)} %bitcast_select_fusion), channel_id=1, source_target_pairs={{0,64},{1,65},{2,66},{3,67},{8,72},{9,73},{10,74},{11,75},{16,80},... | collective-permute-start | bytes 153608 | tf_op jit(solution)/shard_map/ppermute | solution.py:31
  7.9 0.1 collective-permute-done.6
  8.1 6.5 %collective-permute-start.8 = (bf16[80,640]{1,0:T(8,128)(2,1)S(1)}, bf16[80,640]{1,0:T(8,128)(2,1)S(1)}, u32[]{:S(2)}, u32[]{:S(2)}) collective-permute-start(bf16[80,640]{1,0:T(8,128)(2,1)S(1)} %pad_maximum_fusion.2), channel_id=1, source_target_pairs={{0,192},{1,193},{2,194},{3,195},{8,200},{9,201},{10,202},{11,203},... | collective-permute-start | bytes 307208 | tf_op jit(solution)/shard_map/ppermute | solution.py:31
  14.6 0.0 collective-permute-done.5
  14.7 9.6 %collective-permute-start.7 = (bf16[120,640]{1,0:T(8,128)(2,1)S(1)}, bf16[120,640]{1,0:T(8,128)(2,1)S(1)}, u32[]{:S(2)}, u32[]{:S(2)}) collective-permute-start(bf16[120,640]{1,0:T(8,128)(2,1)S(1)} %pad_maximum_fusion.1), channel_id=1, source_target_pairs={{0,324},{1,325},{2,326},{3,327},{8,332},{9,333},{10,334},{11,335},... | collective-permute-start | bytes 460808 | tf_op jit(solution)/shard_map/ppermute | solution.py:31
  24.3 6.9 %collective-permute-done.7 = bf16[120,640]{1,0:T(8,128)(2,1)S(1)} collective-permute-done((bf16[120,640]{1,0:T(8,128)(2,1)S(1)}, bf16[120,640]{1,0:T(8,128)(2,1)S(1)}, u32[]{:S(2)}, u32[]{:S(2)}) %collective-permute-start.7) | collective-permute-done | bytes 153632 | tf_op jit(solution)/shard_map/ppermute | solution.py:31
  31.2 0.0 collective-permute-done.8
  31.3 3.4 %collective-permute-start.11 = (bf16[320,640]{1,0:T(8,128)(2,1)S(1)}, bf16[320,640]{1,0:T(8,128)(2,1)S(1)}, u32[]{:S(2)}, u32[]{:S(2)}) collective-permute-start(bf16[320,640]{1,0:T(8,128)(2,1)S(1)} %constant_dynamic-update-slice_fusion), channel_id=1, source_target_pairs={{0,1},{1,2},{2,3},{3,0},{8,9},{9,10},{10,11},{11,8},{16,17},{17,18... | collective-permute-start | bytes 1228808 | tf_op jit(solution)/shard_map/ppermute | solution.py:31
  34.7 4.6 %collective-permute-start.10 = (bf16[320,640]{1,0:T(8,128)(2,1)S(1)}, bf16[320,640]{1,0:T(8,128)(2,1)S(1)}, u32[]{:S(2)}, u32[]{:S(2)}) collective-permute-start(bf16[320,640]{1,0:T(8,128)(2,1)S(1)} %constant_dynamic-update-slice_fusion), channel_id=1, source_target_pairs={{0,2},{1,3},{2,0},{3,1},{8,10},{9,11},{10,8},{11,9},{16,18},{17,19... | collective-permute-start | bytes 1228808 | tf_op jit(solution)/shard_map/ppermute | solution.py:31
  39.3 3.3 %collective-permute-start.9 = (bf16[320,640]{1,0:T(8,128)(2,1)S(1)}, bf16[320,640]{1,0:T(8,128)(2,1)S(1)}, u32[]{:S(2)}, u32[]{:S(2)}) collective-permute-start(bf16[320,640]{1,0:T(8,128)(2,1)S(1)} %constant_dynamic-update-slice_fusion), channel_id=1, source_target_pairs={{0,3},{1,0},{2,1},{3,2},{8,11},{9,8},{10,9},{11,10},{16,19},{17,16... | collective-permute-start | bytes 1228808 | tf_op jit(solution)/shard_map/ppermute | solution.py:31
  42.7 0.0 collective-permute-done.11
  42.7 5.0 %collective-permute-done.10 = bf16[320,640]{1,0:T(8,128)(2,1)S(1)} collective-permute-done((bf16[320,640]{1,0:T(8,128)(2,1)S(1)}, bf16[320,640]{1,0:T(8,128)(2,1)S(1)}, u32[]{:S(2)}, u32[]{:S(2)}) %collective-permute-start.10) | collective-permute-done | bytes 409632 | tf_op jit(solution)/shard_map/ppermute | solution.py:31
  47.7 1.8 collective-permute-done.9
  49.5 0.2 pad_maximum_fusion.g0
  49.7 0.0 copy-start
  49.7 3.5 %collective-permute-start.14 = (bf16[4,320,640]{2,1,0:T(8,128)(2,1)S(1)}, bf16[4,320,640]{2,1,0:T(8,128)(2,1)}, u32[]{:S(2)}, u32[]{:S(2)}) collective-permute-start(bf16[4,320,640]{2,1,0:T(8,128)(2,1)S(1)} %pad_maximum_fusion.g0), channel_id=1, source_target_pairs={{0,8},{1,9},{2,10},{3,11},{8,16},{9,17},{10,18},{11,19},{16,24},{1... | collective-permute-start | bytes 4915208 | tf_op jit(solution)/shard_map/ppermute | solution.py:31
  53.2 4.8 %collective-permute-start.13 = (bf16[4,320,640]{2,1,0:T(8,128)(2,1)S(1)}, bf16[4,320,640]{2,1,0:T(8,128)(2,1)}, u32[]{:S(2)}, u32[]{:S(2)}) collective-permute-start(bf16[4,320,640]{2,1,0:T(8,128)(2,1)S(1)} %pad_maximum_fusion.g0), channel_id=1, source_target_pairs={{0,16},{1,17},{2,18},{3,19},{8,24},{9,25},{10,26},{11,27},{16,0},{... | collective-permute-start | bytes 4915208 | tf_op jit(solution)/shard_map/ppermute | solution.py:31
  58.0 3.3 %collective-permute-start.12 = (bf16[4,320,640]{2,1,0:T(8,128)(2,1)S(1)}, bf16[4,320,640]{2,1,0:T(8,128)(2,1)}, u32[]{:S(2)}, u32[]{:S(2)}) collective-permute-start(bf16[4,320,640]{2,1,0:T(8,128)(2,1)S(1)} %pad_maximum_fusion.g0), channel_id=1, source_target_pairs={{0,24},{1,25},{2,26},{3,27},{8,0},{9,1},{10,2},{11,3},{16,8},{17,9... | collective-permute-start | bytes 4915208 | tf_op jit(solution)/shard_map/ppermute | solution.py:31
  61.3 0.0 copy-done.1
  61.3 8.9 %collective-permute-start.1 = (bf16[512,640]{1,0:T(8,128)(2,1)S(1)}, bf16[512,640]{1,0:T(8,128)(2,1)S(1)}, u32[]{:S(2)}, u32[]{:S(2)}) collective-permute-start(bf16[512,640]{1,0:T(8,128)(2,1)S(1)} %copy-done.1), channel_id=1, source_target_pairs={{0,4},{1,5},{2,6},{3,7},{4,8},{5,9},{6,10},{7,11},{8,12},{9,13},{1... | collective-permute-start | bytes 1966088 | tf_op jit(solution)/shard_map/ppermute | solution.py:36
  70.2 5.0 %collective-permute-start.3 = (bf16[128,640]{1,0:T(8,128)(2,1)S(1)}, bf16[128,640]{1,0:T(8,128)(2,1)S(1)}, u32[]{:S(2)}, u32[]{:S(2)}) collective-permute-start(bf16[128,640]{1,0:T(8,128)(2,1)S(1)} %slice.8), channel_id=1, source_target_pairs={{0,2},{1,3},{2,8},{3,9},{4,6},{5,7},{6,12},{7,13},{8,10},{9,11},{1... | collective-permute-start | bytes 491528 | tf_op jit(solution)/shard_map/ppermute | solution.py:36
  75.2 38.1 %collective-permute-done.3.ts_ref = bf16[128,640]{1,0:T(8,128)(2,1)S(1)} collective-permute-done((bf16[128,640]{1,0:T(8,128)(2,1)S(1)}, bf16[128,640]{1,0:T(8,128)(2,1)S(1)}, u32[]{:S(2)}, u32[]{:S(2)}) %collective-permute-start.3) | collective-permute-done | bytes 163872 | tf_op jit(solution)/shard_map/ppermute | solution.py:36
  113.3 1.9 collective-permute-start.15
  115.2 0.0 collective-permute-done.14.g3
  115.2 2.4 %collective-permute-start.18 = (bf16[4,320,640]{2,1,0:T(8,128)(2,1)}, bf16[4,320,640]{2,1,0:T(8,128)(2,1)}, u32[]{:S(2)}, u32[]{:S(2)}) collective-permute-start(bf16[4,320,640]{2,1,0:T(8,128)(2,1)} %collective-permute-done.14.g3), channel_id=1, source_target_pairs={{0,32},{1,33},{2,34},{3,35},{8,40},{9,41},{10,42},{11,43},{16,48},... | collective-permute-start | bytes 4915208 | tf_op jit(solution)/shard_map/ppermute | solution.py:31
  117.6 0.0 collective-permute-done.13.g2
  117.6 1.9 collective-permute-start.17
  119.6 0.0 collective-permute-done.12.g1
  119.6 2.4 %collective-permute-start.16 = (bf16[4,320,640]{2,1,0:T(8,128)(2,1)}, bf16[4,320,640]{2,1,0:T(8,128)(2,1)}, u32[]{:S(2)}, u32[]{:S(2)}) collective-permute-start(bf16[4,320,640]{2,1,0:T(8,128)(2,1)} %collective-permute-done.12.g1), channel_id=1, source_target_pairs={{0,32},{1,33},{2,34},{3,35},{8,40},{9,41},{10,42},{11,43},{16,48},... | collective-permute-start | bytes 4915208 | tf_op jit(solution)/shard_map/ppermute | solution.py:31
  122.0 27.2 %collective-permute-done.1.r_ref = bf16[512,640]{1,0:T(8,128)(2,1)S(1)} collective-permute-done((bf16[512,640]{1,0:T(8,128)(2,1)S(1)}, bf16[512,640]{1,0:T(8,128)(2,1)S(1)}, u32[]{:S(2)}, u32[]{:S(2)}) %collective-permute-start.1) | collective-permute-done | bytes 655392 | tf_op jit(solution)/shard_map/ppermute | solution.py:36
  149.2 1.9 collective-permute-start
  151.2 15.9 %collective-permute-done.a_ref = bf16[512,640]{1,0:T(8,128)(2,1)S(1)} collective-permute-done((bf16[512,640]{1,0:T(8,128)(2,1)S(1)}, bf16[512,640]{1,0:T(8,128)(2,1)S(1)}, u32[]{:S(2)}, u32[]{:S(2)}) %collective-permute-start) | collective-permute-done | bytes 655392 | tf_op jit(solution)/shard_map/ppermute | solution.py:36
  167.1 1.9 collective-permute-start.4
  169.0 6.8 %collective-permute-done.4.tr_ref = bf16[128,640]{1,0:T(8,128)(2,1)S(1)} collective-permute-done((bf16[128,640]{1,0:T(8,128)(2,1)S(1)}, bf16[128,640]{1,0:T(8,128)(2,1)S(1)}, u32[]{:S(2)}, u32[]{:S(2)}) %collective-permute-start.4) | collective-permute-done | bytes 163872 | tf_op jit(solution)/shard_map/ppermute | solution.py:31
  175.8 0.0 copy-done.3
  175.8 1.9 collective-permute-start.2
  177.8 0.7 stack.66.where
  178.4 0.1 compare_reduce_fusion
  178.5 0.1 fusion.9
  178.5 1.1 fusion.perm_ref
  179.7 9.9 %collective-permute-done.2.b_ref = bf16[512,640]{1,0:T(8,128)(2,1)} collective-permute-done((bf16[512,640]{1,0:T(8,128)(2,1)S(1)}, bf16[512,640]{1,0:T(8,128)(2,1)}, u32[]{:S(2)}, u32[]{:S(2)}) %collective-permute-start.2) | collective-permute-done | bytes 655392 | tf_op jit(solution)/shard_map/ppermute | solution.py:31
  189.6 0.0 collective-permute-done.15.h0
  189.6 0.0 collective-permute-done.18.h3
  189.6 0.0 collective-permute-done.17.h2
  189.6 0.0 collective-permute-done.16.h1
  189.7 35.2 %shard_map.64 = bf16[512,640]{1,0:T(8,128)(2,1)} custom-call(s32[8]{0:T(128)} %stack.66.where, bf16[512,640]{1,0:T(8,128)(2,1)} %s_ref.1, bf16[512,640]{1,0:T(8,128)(2,1)} %copy-done.3, bf16[512,640]{1,0:T(8,128)(2,1)} %copy-done.2, bf16[512,640]{1,0:T(8,128)(2,1)} %collective-permute-done.2.b_ref, bf16[128,640]{1,0:T(8,128)(2,1)} %copy-done.4, ...), custom_call_target="tpu_custom_call" | custom-call | flops 15000000512 | bytes 16000000 | tf_op jit(solution)/shard_map/pallas_call | solution.py:162
  (19 shorter events, 0.2 us)
Async XLA Ops:
  0.9 7.2 %collective-permute-start.6 = (bf16[40,640]{1,0:T(8,128)(2,1)S(1)}, bf16[40,640]{1,0:T(8,128)(2,1)S(1)}, u32[]{:S(2)}, u32[]{:S(2)}) collective-permute-start(bf16[40,640]{1,0:T(8,128)(2,1)S(1)} %bitcast_select_fusion), channel_id=1, source_target_pairs={{0,452},{1,453},{2,454},{3,455},{8,460},{9,461},{10,462},{11,463},... | collective-permute-start | bytes 153608 | tf_op jit(solution)/shard_map/ppermute | solution.py:31
  2.9 11.7 %collective-permute-start.5 = (bf16[40,640]{1,0:T(8,128)(2,1)S(1)}, bf16[40,640]{1,0:T(8,128)(2,1)S(1)}, u32[]{:S(2)}, u32[]{:S(2)}) collective-permute-start(bf16[40,640]{1,0:T(8,128)(2,1)S(1)} %bitcast_select_fusion), channel_id=1, source_target_pairs={{0,64},{1,65},{2,66},{3,67},{8,72},{9,73},{10,74},{11,75},{16,80},... | collective-permute-start | bytes 153608 | tf_op jit(solution)/shard_map/ppermute | solution.py:31
  8.1 23.1 %collective-permute-start.8 = (bf16[80,640]{1,0:T(8,128)(2,1)S(1)}, bf16[80,640]{1,0:T(8,128)(2,1)S(1)}, u32[]{:S(2)}, u32[]{:S(2)}) collective-permute-start(bf16[80,640]{1,0:T(8,128)(2,1)S(1)} %pad_maximum_fusion.2), channel_id=1, source_target_pairs={{0,192},{1,193},{2,194},{3,195},{8,200},{9,201},{10,202},{11,203},... | collective-permute-start | bytes 307208 | tf_op jit(solution)/shard_map/ppermute | solution.py:31
  14.7 16.5 %collective-permute-start.7 = (bf16[120,640]{1,0:T(8,128)(2,1)S(1)}, bf16[120,640]{1,0:T(8,128)(2,1)S(1)}, u32[]{:S(2)}, u32[]{:S(2)}) collective-permute-start(bf16[120,640]{1,0:T(8,128)(2,1)S(1)} %pad_maximum_fusion.1), channel_id=1, source_target_pairs={{0,324},{1,325},{2,326},{3,327},{8,332},{9,333},{10,334},{11,335},... | collective-permute-start | bytes 460808 | tf_op jit(solution)/shard_map/ppermute | solution.py:31
  31.3 11.4 %collective-permute-start.11 = (bf16[320,640]{1,0:T(8,128)(2,1)S(1)}, bf16[320,640]{1,0:T(8,128)(2,1)S(1)}, u32[]{:S(2)}, u32[]{:S(2)}) collective-permute-start(bf16[320,640]{1,0:T(8,128)(2,1)S(1)} %constant_dynamic-update-slice_fusion), channel_id=1, source_target_pairs={{0,1},{1,2},{2,3},{3,0},{8,9},{9,10},{10,11},{11,8},{16,17},{17,18... | collective-permute-start | bytes 1228808 | tf_op jit(solution)/shard_map/ppermute | solution.py:31
  34.7 13.0 %collective-permute-start.10 = (bf16[320,640]{1,0:T(8,128)(2,1)S(1)}, bf16[320,640]{1,0:T(8,128)(2,1)S(1)}, u32[]{:S(2)}, u32[]{:S(2)}) collective-permute-start(bf16[320,640]{1,0:T(8,128)(2,1)S(1)} %constant_dynamic-update-slice_fusion), channel_id=1, source_target_pairs={{0,2},{1,3},{2,0},{3,1},{8,10},{9,11},{10,8},{11,9},{16,18},{17,19... | collective-permute-start | bytes 1228808 | tf_op jit(solution)/shard_map/ppermute | solution.py:31
  39.3 10.2 %collective-permute-start.9 = (bf16[320,640]{1,0:T(8,128)(2,1)S(1)}, bf16[320,640]{1,0:T(8,128)(2,1)S(1)}, u32[]{:S(2)}, u32[]{:S(2)}) collective-permute-start(bf16[320,640]{1,0:T(8,128)(2,1)S(1)} %constant_dynamic-update-slice_fusion), channel_id=1, source_target_pairs={{0,3},{1,0},{2,1},{3,2},{8,11},{9,8},{10,9},{11,10},{16,19},{17,16... | collective-permute-start | bytes 1228808 | tf_op jit(solution)/shard_map/ppermute | solution.py:31
  49.5 11.8 %copy-start.1 = (bf16[512,640]{1,0:T(8,128)(2,1)S(1)}, bf16[512,640]{1,0:T(8,128)(2,1)}, u32[]{:S(2)}) copy-start(bf16[512,640]{1,0:T(8,128)(2,1)} %s_ref.1) | copy-start | bytes 1966084
  49.7 139.9 %copy-start = (bf16[4,320,640]{2,1,0:T(8,128)(2,1)}, bf16[4,320,640]{2,1,0:T(8,128)(2,1)S(1)}, u32[]{:S(2)}) copy-start(bf16[4,320,640]{2,1,0:T(8,128)(2,1)S(1)} %pad_maximum_fusion.g0) | copy-start | bytes 4915204
  49.7 65.5 %collective-permute-start.14 = (bf16[4,320,640]{2,1,0:T(8,128)(2,1)S(1)}, bf16[4,320,640]{2,1,0:T(8,128)(2,1)}, u32[]{:S(2)}, u32[]{:S(2)}) collective-permute-start(bf16[4,320,640]{2,1,0:T(8,128)(2,1)S(1)} %pad_maximum_fusion.g0), channel_id=1, source_target_pairs={{0,8},{1,9},{2,10},{3,11},{8,16},{9,17},{10,18},{11,19},{16,24},{1... | collective-permute-start | bytes 4915208 | tf_op jit(solution)/shard_map/ppermute | solution.py:31
  53.2 64.4 %collective-permute-start.13 = (bf16[4,320,640]{2,1,0:T(8,128)(2,1)S(1)}, bf16[4,320,640]{2,1,0:T(8,128)(2,1)}, u32[]{:S(2)}, u32[]{:S(2)}) collective-permute-start(bf16[4,320,640]{2,1,0:T(8,128)(2,1)S(1)} %pad_maximum_fusion.g0), channel_id=1, source_target_pairs={{0,16},{1,17},{2,18},{3,19},{8,24},{9,25},{10,26},{11,27},{16,0},{... | collective-permute-start | bytes 4915208 | tf_op jit(solution)/shard_map/ppermute | solution.py:31
  58.0 61.5 %collective-permute-start.12 = (bf16[4,320,640]{2,1,0:T(8,128)(2,1)S(1)}, bf16[4,320,640]{2,1,0:T(8,128)(2,1)}, u32[]{:S(2)}, u32[]{:S(2)}) collective-permute-start(bf16[4,320,640]{2,1,0:T(8,128)(2,1)S(1)} %pad_maximum_fusion.g0), channel_id=1, source_target_pairs={{0,24},{1,25},{2,26},{3,27},{8,0},{9,1},{10,2},{11,3},{16,8},{17,9... | collective-permute-start | bytes 4915208 | tf_op jit(solution)/shard_map/ppermute | solution.py:31
  61.3 87.9 %collective-permute-start.1 = (bf16[512,640]{1,0:T(8,128)(2,1)S(1)}, bf16[512,640]{1,0:T(8,128)(2,1)S(1)}, u32[]{:S(2)}, u32[]{:S(2)}) collective-permute-start(bf16[512,640]{1,0:T(8,128)(2,1)S(1)} %copy-done.1), channel_id=1, source_target_pairs={{0,4},{1,5},{2,6},{3,7},{4,8},{5,9},{6,10},{7,11},{8,12},{9,13},{1... | collective-permute-start | bytes 1966088 | tf_op jit(solution)/shard_map/ppermute | solution.py:36
  70.2 43.0 %collective-permute-start.3 = (bf16[128,640]{1,0:T(8,128)(2,1)S(1)}, bf16[128,640]{1,0:T(8,128)(2,1)S(1)}, u32[]{:S(2)}, u32[]{:S(2)}) collective-permute-start(bf16[128,640]{1,0:T(8,128)(2,1)S(1)} %slice.8), channel_id=1, source_target_pairs={{0,2},{1,3},{2,8},{3,9},{4,6},{5,7},{6,12},{7,13},{8,10},{9,11},{1... | collective-permute-start | bytes 491528 | tf_op jit(solution)/shard_map/ppermute | solution.py:36
  113.3 76.4 %copy-start.4 = (bf16[128,640]{1,0:T(8,128)(2,1)}, bf16[128,640]{1,0:T(8,128)(2,1)S(1)}, u32[]{:S(2)}) copy-start(bf16[128,640]{1,0:T(8,128)(2,1)S(1)} %collective-permute-done.3.ts_ref) | copy-start | bytes 491524
  113.3 76.3 %collective-permute-start.15 = (bf16[4,320,640]{2,1,0:T(8,128)(2,1)S(1)}, bf16[4,320,640]{2,1,0:T(8,128)(2,1)}, u32[]{:S(2)}, u32[]{:S(2)}) collective-permute-start(bf16[4,320,640]{2,1,0:T(8,128)(2,1)S(1)} %pad_maximum_fusion.g0), channel_id=1, source_target_pairs={{0,32},{1,33},{2,34},{3,35},{8,40},{9,41},{10,42},{11,43},{16,48},... | collective-permute-start | bytes 4915208 | tf_op jit(solution)/shard_map/ppermute | solution.py:31
  115.2 74.4 %collective-permute-start.18 = (bf16[4,320,640]{2,1,0:T(8,128)(2,1)}, bf16[4,320,640]{2,1,0:T(8,128)(2,1)}, u32[]{:S(2)}, u32[]{:S(2)}) collective-permute-start(bf16[4,320,640]{2,1,0:T(8,128)(2,1)} %collective-permute-done.14.g3), channel_id=1, source_target_pairs={{0,32},{1,33},{2,34},{3,35},{8,40},{9,41},{10,42},{11,43},{16,48},... | collective-permute-start | bytes 4915208 | tf_op jit(solution)/shard_map/ppermute | solution.py:31
  117.6 72.0 %collective-permute-start.17 = (bf16[4,320,640]{2,1,0:T(8,128)(2,1)}, bf16[4,320,640]{2,1,0:T(8,128)(2,1)}, u32[]{:S(2)}, u32[]{:S(2)}) collective-permute-start(bf16[4,320,640]{2,1,0:T(8,128)(2,1)} %collective-permute-done.13.g2), channel_id=1, source_target_pairs={{0,32},{1,33},{2,34},{3,35},{8,40},{9,41},{10,42},{11,43},{16,48},... | collective-permute-start | bytes 4915208 | tf_op jit(solution)/shard_map/ppermute | solution.py:31
  119.6 70.0 %collective-permute-start.16 = (bf16[4,320,640]{2,1,0:T(8,128)(2,1)}, bf16[4,320,640]{2,1,0:T(8,128)(2,1)}, u32[]{:S(2)}, u32[]{:S(2)}) collective-permute-start(bf16[4,320,640]{2,1,0:T(8,128)(2,1)} %collective-permute-done.12.g1), channel_id=1, source_target_pairs={{0,32},{1,33},{2,34},{3,35},{8,40},{9,41},{10,42},{11,43},{16,48},... | collective-permute-start | bytes 4915208 | tf_op jit(solution)/shard_map/ppermute | solution.py:31
  149.2 40.4 %copy-start.2 = (bf16[512,640]{1,0:T(8,128)(2,1)}, bf16[512,640]{1,0:T(8,128)(2,1)S(1)}, u32[]{:S(2)}) copy-start(bf16[512,640]{1,0:T(8,128)(2,1)S(1)} %collective-permute-done.1.r_ref) | copy-start | bytes 1966084
  149.2 17.9 %collective-permute-start = (bf16[512,640]{1,0:T(8,128)(2,1)S(1)}, bf16[512,640]{1,0:T(8,128)(2,1)S(1)}, u32[]{:S(2)}, u32[]{:S(2)}) collective-permute-start(bf16[512,640]{1,0:T(8,128)(2,1)S(1)} %copy-done.1), channel_id=1, source_target_pairs={{0,1},{1,2},{2,3},{3,8},{4,5},{5,6},{6,7},{7,12},{8,9},{9,10},{10,... | collective-permute-start | bytes 1966088 | tf_op jit(solution)/shard_map/ppermute | solution.py:36
  167.1 8.7 %copy-start.3 = (bf16[512,640]{1,0:T(8,128)(2,1)}, bf16[512,640]{1,0:T(8,128)(2,1)S(1)}, u32[]{:S(2)}) copy-start(bf16[512,640]{1,0:T(8,128)(2,1)S(1)} %collective-permute-done.a_ref) | copy-start | bytes 1966084
  167.1 8.7 %collective-permute-start.4 = (bf16[128,640]{1,0:T(8,128)(2,1)S(1)}, bf16[128,640]{1,0:T(8,128)(2,1)S(1)}, u32[]{:S(2)}, u32[]{:S(2)}) collective-permute-start(bf16[128,640]{1,0:T(8,128)(2,1)S(1)} %slice.19), channel_id=1, source_target_pairs={{0,2},{1,3},{2,0},{3,1},{8,10},{9,11},{10,8},{11,9},{16,18},{17,19... | collective-permute-start | bytes 491528 | tf_op jit(solution)/shard_map/ppermute | solution.py:31
  175.8 13.8 %copy-start.5 = (bf16[128,640]{1,0:T(8,128)(2,1)}, bf16[128,640]{1,0:T(8,128)(2,1)S(1)}, u32[]{:S(2)}) copy-start(bf16[128,640]{1,0:T(8,128)(2,1)S(1)} %collective-permute-done.4.tr_ref) | copy-start | bytes 491524
  175.8 13.8 %collective-permute-start.2 = (bf16[512,640]{1,0:T(8,128)(2,1)S(1)}, bf16[512,640]{1,0:T(8,128)(2,1)}, u32[]{:S(2)}, u32[]{:S(2)}) collective-permute-start(bf16[512,640]{1,0:T(8,128)(2,1)S(1)} %collective-permute-done.1.r_ref), channel_id=1, source_target_pairs={{0,1},{1,2},{2,3},{3,0},{8,9},{9,10},{10,11},{11,8},{16,17},{17,18... | collective-permute-start | bytes 1966088 | tf_op jit(solution)/shard_map/ppermute | solution.py:31

commit v2 on v1

v2 whole, which is shorter than its diff:
```python
import jax
import jax.numpy as jnp
from jax import lax
from jax.experimental import pallas as pl
from jax.experimental.pallas import tpu as pltpu
from jax.sharding import Mesh
from jax.sharding import PartitionSpec as P

D = 640
LAYERS = 3
BLOCK = 512
TAIL = 128
AXES = ("zl", "core", "y", "zh", "x")
SIZES = (8, 2, 4, 2, 4)
DEVICES = 512
Z_SLOTS = (-1, 0, 1, 2, 3, 4, -3, -2)


def index_of(z, core, y, x):
    z, y, x = z % 16, y % 4, x % 4
    return (((z % 8) * 2 + core) * 4 + y) * 8 + (z // 8) * 4 + x


def permuted(value, target):
    pairs = []
    for z in range(16):
        for core in range(2):
            for y in range(4):
                for x in range(4):
                    pairs.append((index_of(z, core, y, x), index_of(*target(z, core, y, x))))
    return lax.ppermute(value, AXES, pairs)


def shifted(value, target):
    pairs = [(b, target(b)) for b in range(DEVICES)]
    return lax.ppermute(value, AXES, [(a, b) for a, b in pairs if b < DEVICES])


def from_z(value, by):
    return permuted(value, lambda z, core, y, x: (z - by, core, y, x))


def normed(values):
    scale = lax.rsqrt(jnp.mean(values * values, axis=1, keepdims=True) + 1e-06)
    return (values * scale).astype(jnp.bfloat16)


def kernel(
    where, s_ref, a_ref, r_ref, b_ref, ts_ref, tr_ref, perm_ref, bias_ref,
    gathered, out_ref, taps, mix, x0, u1, u2, x1, u3, sems,
):
    x = where[0]

    def fetch(px, py, target, sem):
        for half in range(2):
            pltpu.make_async_copy(gathered.at[half * 16 + py * 4 + px], target(half * 320), sem).start()

    def fetch_mix(layer):
        fetch(layer, 3, lambda row: mix.at[layer, pl.ds(row, 320)], sems.at[3 + layer])

    def fetch_taps(layer):
        for px in range(4):
            rows, columns = (px // 2) * D, pl.ds((px % 2) * D, D)
            fetch(px, layer, lambda row: taps.at[layer, pl.ds(rows + row, 320), columns], sems.at[layer])

    for index in range(LAYERS):
        fetch_taps(index)
        fetch_mix(index)

    def ready(layer):
        pltpu.make_async_copy(taps.at[layer], taps.at[layer], sems.at[layer]).wait()
        pltpu.make_async_copy(mix.at[layer], mix.at[layer], sems.at[3 + layer]).wait()

    def bring(ref, slot, tail_slot):
        exact = jnp.dot(ref[...], perm_ref[...], preferred_element_type=jnp.float32)
        x0[slot] = exact.astype(jnp.bfloat16)
        unit = normed(exact)
        u1[slot, TAIL:] = unit
        if tail_slot is not None:
            u1[tail_slot, :TAIL] = unit[BLOCK - TAIL :]

    def bring_tail(ref, slot):
        exact = jnp.dot(ref[...], perm_ref[...], preferred_element_type=jnp.float32)
        u1[slot, :TAIL] = normed(exact)

    a_slot = jnp.where(x == 0, 0, 2)
    t_slot = jnp.where(x < 2, 0, 2)
    bring(s_ref, 3, None)
    bring(r_ref, 1, None)
    bring(a_ref, a_slot, a_slot + 1)
    bring(b_ref, 2 - a_slot, 3 - a_slot)
    bring_tail(ts_ref, t_slot)
    bring_tail(tr_ref, 2 - t_slot)

    def layer(prev, now, held, index):
        both = jnp.concatenate([prev, now], axis=1)
        pre = jnp.dot(both, taps[index], preferred_element_type=jnp.float32)
        pre = pre + bias_ref[index : index + 1, :]
        hidden = (pre[:, :D] * jax.nn.sigmoid(pre[:, D:])).astype(jnp.bfloat16)
        return held + lax.dot_general(
            hidden, mix[index], (((1,), (1,)), ((), ())), preferred_element_type=jnp.float32
        )

    ready(0)

    def keep(slot, unit):
        return jnp.where(where[1 + slot] != 0, unit, jnp.zeros_like(unit))

    def two(ref, first, second, rows):
        return jnp.concatenate([ref[first, rows], ref[second, rows]], axis=0)

    def first_layer(pair):
        low, high = 2 * pair, 2 * pair + 1
        prev = two(u1, low, high, pl.ds(0, BLOCK))
        now = two(u1, low, high, pl.ds(TAIL, BLOCK))
        after = layer(prev, now, two(x0, low, high, pl.ds(0, BLOCK)).astype(jnp.float32), 0)
        unit = normed(after)
        u2[low] = keep(low, unit[:BLOCK])
        u2[high] = keep(high, unit[BLOCK:])
        x1[pair] = after[BLOCK:]

    pl.loop(0, 2)(first_layer)

    ready(1)
    after = layer(two(u2, 0, 2, slice(None)), two(u2, 1, 3, slice(None)), jnp.concatenate([x1[0], x1[1]], axis=0), 1)
    unit = normed(after)
    u3[0] = keep(1, unit[:BLOCK])
    u3[1] = unit[BLOCK:]
    x1[1] = after[BLOCK:]

    ready(2)
    after = layer(u3[0], u3[1], x1[1], 2).astype(jnp.bfloat16)
    out_ref[...] = lax.dot_general(
        after, perm_ref[...], (((1,), (1,)), ((), ())), preferred_element_type=jnp.float32
    ).astype(jnp.bfloat16)


def block_output(where, rows_in, perm, bias, weights):
    vmem = pl.BlockSpec(memory_space=pltpu.VMEM)
    hbm = pl.BlockSpec(memory_space=pl.ANY)
    return pl.pallas_call(
        kernel,
        out_shape=jax.ShapeDtypeStruct((BLOCK, D), jnp.bfloat16),
        in_specs=[pl.BlockSpec(memory_space=pltpu.SMEM)] + [vmem] * 8 + [hbm],
        out_specs=vmem,
        scratch_shapes=[
            pltpu.VMEM((3, 2 * D, 2 * D), jnp.bfloat16),
            pltpu.VMEM((3, D, D), jnp.bfloat16),
            pltpu.VMEM((4, BLOCK, D), jnp.bfloat16),
            pltpu.VMEM((4, TAIL + BLOCK, D), jnp.bfloat16),
            pltpu.VMEM((4, BLOCK, D), jnp.bfloat16),
            pltpu.VMEM((2, BLOCK, D), jnp.float32),
            pltpu.VMEM((2, BLOCK, D), jnp.bfloat16),
            pltpu.SemaphoreType.DMA((6,)),
        ],
        compiler_params=pltpu.CompilerParams(vmem_limit_bytes=56 * 1024 * 1024),
        cost_estimate=pl.CostEstimate(flops=15_000_000_000, bytes_accessed=16_000_000, transcendentals=3_000_000),
    )(where, *rows_in, perm, bias, weights)


def local(sequence_input, w_prev, w_now, conv_bias, w_mix):
    zl, core, y, zh, x = (lax.axis_index(a) for a in AXES)
    block = (((zl * 2 + core) * 4 + y) * 2 + zh) * 4 + x

    at = jnp.minimum(y, 2)
    tap_prev = lax.dynamic_slice(w_prev, (at, 0, (x % 2) * D), (1, 40, D))[0]
    tap_now = lax.dynamic_slice(w_now, (at, 0, (x % 2) * D), (1, 40, D))[0]
    mixing = lax.dynamic_slice(w_mix, (jnp.minimum(x, 2), 0, 0), (1, D, 40))[0].T
    piece = jnp.where(y == 3, mixing, jnp.where(x < 2, tap_prev, tap_now))

    own = sequence_input
    stepped = lax.ppermute(
        own, AXES, [(b, b + 8) for b in range(DEVICES) if b % 8 >= 4 and b + 8 < DEVICES]
    )
    above, below = from_z(piece, 1), from_z(piece, -1)
    three = jnp.concatenate([below, piece, above])
    far_above, far_below = from_z(three, 3), from_z(three[40:], -3)
    near = jnp.concatenate([three, far_above, far_below])

    k = jnp.arange(D)
    shard = (zl + jnp.asarray(Z_SLOTS, jnp.int32)[(k % 320) // 40]) % 8
    channel = (shard * 2 + k // 320) * 40 + k % 40
    perm = (k[:, None] == channel[None, :]).astype(jnp.bfloat16)
    where = jnp.stack([x, block >= 5, block >= 4, block >= 1, block >= 0]).astype(jnp.int32)
    near, own, stepped, perm, where = lax.optimization_barrier((near, own, stepped, perm, where))

    weights = lax.all_gather(near, ("core", "y", "x"))
    far = permuted(
        jnp.where(zh == 1, stepped, own), lambda z, c, yy, xx: (z + 8, c, yy, xx)
    )
    beside = shifted(own, lambda b: b + 1 if b % 4 < 3 else b + 5)
    own_tail = shifted(own[BLOCK - TAIL :], lambda b: b + 2 if b % 4 < 2 else b + 6)
    far, beside, own_tail = lax.optimization_barrier((far, beside, own_tail))
    far_beside = permuted(far, lambda z, c, yy, xx: (z, c, yy, xx + 1))
    far_tail = permuted(far[BLOCK - TAIL :], lambda z, c, yy, xx: (z, c, yy, xx + 2))

    rows_in = (own, beside, far, far_beside, own_tail, far_tail)
    return block_output(where, rows_in, perm, conv_bias, weights)


def solution(mesh):
    finer = Mesh(mesh.devices.reshape(SIZES), AXES)
    seqa, seqb = AXES[:2], AXES[2:]
    in_specs = (P(AXES, None), P(None, seqa, None), P(None, seqa, None), P(), P(None, None, seqa))
    return jax.shard_map(
        local, mesh=finer, in_specs=in_specs, out_specs=P(AXES, None), check_vma=False
    )
```

time: 226 us -> 187 us (0.83)
  the two profiles are of different devices: /device:TPU:96 before, /device:TPU:121 now
where the time goes in v2:
time: 187 us
  waiting for transfers between devices  103 us (55%)
  starting transfers between devices  37.9 us (20%)
  Pallas kernels  28.4 us (15%)
  between operations  13.6 us (7%)
  other arithmetic  2.32 us (1%)
    ppermute x7, waiting for transfers between devices, permuted(): return lax.ppermute(value, AXES, pairs)  81.4 us
    ppermute x7, starting transfers between devices, permuted(): return lax.ppermute(value, AXES, pairs)  29.7 us
    pallas_call x1, Pallas kernels, block_output(): pl.pallas_call(kernel, out_shape=jax.ShapeDtypeStruct((BLOCK, D), jnp.bfl...  28.4 us
    ppermute x2, waiting for transfers between devices, shifted(): return lax.ppermute(value, AXES, [(a, b) for a, b in pairs if b < DEVICES])  19.6 us
    ppermute x2, starting transfers between devices, shifted(): return lax.ppermute(value, AXES, [(a, b) for a, b in pairs if b < DEVICES])  7.48 us
  transfers between devices with their start and end apart: 11, of which 6 were waited for; matrix products, arithmetic and copies ran while one was open for 1% of the time, Pallas kernels for 0%

profile of v2, /device:TPU:121, one launch (start us, length us, event | category | flops | bytes accessed | tf_op | source)
XLA Modules:
  0.0 186.6 jit_solution(8050833263123710319)
XLA Ops:
  6.5 0.0 copy-start
  6.5 0.0 all-gather.3.cloned.1.call-start
  6.5 0.9 bitcast_select_fusion
  7.5 1.9 %collective-permute-start.1 = (bf16[40,640]{1,0:T(8,128)(2,1)S(1)}, bf16[40,640]{1,0:T(8,128)(2,1)S(1)}, u32[]{:S(2)}, u32[]{:S(2)}) collective-permute-start(bf16[40,640]{1,0:T(8,128)(2,1)S(1)} %bitcast_select_fusion), channel_id=1, source_target_pairs={{0,452},{1,453},{2,454},{3,455},{8,460},{9,461},{10,462},{11,463},... | collective-permute-start | bytes 153608 | tf_op jit(solution)/shard_map/ppermute | solution.py:31
  9.4 4.8 %collective-permute-start = (bf16[40,640]{1,0:T(8,128)(2,1)S(1)}, bf16[40,640]{1,0:T(8,128)(2,1)S(1)}, u32[]{:S(2)}, u32[]{:S(2)}) collective-permute-start(bf16[40,640]{1,0:T(8,128)(2,1)S(1)} %bitcast_select_fusion), channel_id=1, source_target_pairs={{0,64},{1,65},{2,66},{3,67},{8,72},{9,73},{10,74},{11,75},{16,80},... | collective-permute-start | bytes 153608 | tf_op jit(solution)/shard_map/ppermute | solution.py:31
  14.2 0.7 collective-permute-start.4
  14.9 0.1 compare_reduce_fusion
  14.9 0.1 fusion.12
  15.0 1.1 fusion.perm_ref
  16.2 0.6 stack.39.where
  16.7 0.0 collective-permute-done.1
  16.8 6.3 %collective-permute-start.3 = (bf16[80,640]{1,0:T(8,128)(2,1)S(1)}, bf16[80,640]{1,0:T(8,128)(2,1)S(1)}, u32[]{:S(2)}, u32[]{:S(2)}) collective-permute-start(bf16[80,640]{1,0:T(8,128)(2,1)S(1)} %pad_maximum_fusion.1), channel_id=1, source_target_pairs={{0,192},{1,193},{2,194},{3,195},{8,200},{9,201},{10,202},{11,203},... | collective-permute-start | bytes 307208 | tf_op jit(solution)/shard_map/ppermute | solution.py:31
  23.0 0.0 collective-permute-done
  23.1 2.9 %collective-permute-start.2 = (bf16[120,640]{1,0:T(8,128)(2,1)S(1)}, bf16[120,640]{1,0:T(8,128)(2,1)S(1)}, u32[]{:S(2)}, u32[]{:S(2)}) collective-permute-start(bf16[120,640]{1,0:T(8,128)(2,1)S(1)} %pad_maximum_fusion), channel_id=1, source_target_pairs={{0,324},{1,325},{2,326},{3,327},{8,332},{9,333},{10,334},{11,335},... | collective-permute-start | bytes 460808 | tf_op jit(solution)/shard_map/ppermute | solution.py:31
  26.0 17.2 %collective-permute-done.2 = bf16[120,640]{1,0:T(8,128)(2,1)S(1)} collective-permute-done((bf16[120,640]{1,0:T(8,128)(2,1)S(1)}, bf16[120,640]{1,0:T(8,128)(2,1)S(1)}, u32[]{:S(2)}, u32[]{:S(2)}) %collective-permute-start.2) | collective-permute-done | bytes 153632 | tf_op jit(solution)/shard_map/ppermute | solution.py:31
  43.2 0.0 collective-permute-done.3
  43.2 0.0 copy-start.1
  43.2 0.0 collective-permute-done.4
  43.2 0.7 copy-done.1
  44.0 0.0 all-gather.3.cloned.1.call-update
  44.0 0.0 copy-done
  44.0 0.1 broadcast_select_fusion
  44.1 6.4 %collective-permute-start.5 = (bf16[512,640]{1,0:T(8,128)(2,1)S(1)}, bf16[512,640]{1,0:T(8,128)(2,1)S(1)}, u32[]{:S(2)}, u32[]{:S(2)}) collective-permute-start(bf16[512,640]{1,0:T(8,128)(2,1)S(1)} %broadcast_select_fusion), channel_id=1, source_target_pairs={{0,4},{1,5},{2,6},{3,7},{8,12},{9,13},{10,14},{11,15},{16,20},{17,... | collective-permute-start | bytes 1966088 | tf_op jit(solution)/shard_map/ppermute | solution.py:31
  50.5 3.1 %collective-permute-start.6 = (bf16[512,640]{1,0:T(8,128)(2,1)S(1)}, bf16[512,640]{1,0:T(8,128)(2,1)S(1)}, u32[]{:S(2)}, u32[]{:S(2)}) collective-permute-start(bf16[512,640]{1,0:T(8,128)(2,1)S(1)} %copy-done), channel_id=1, source_target_pairs={{0,1},{1,2},{2,3},{3,8},{4,5},{5,6},{6,7},{7,12},{8,9},{9,10},{10,... | collective-permute-start | bytes 1966088 | tf_op jit(solution)/shard_map/ppermute | solution.py:36
  53.6 4.4 %collective-permute-start.7 = (bf16[128,640]{1,0:T(8,128)(2,1)S(1)}, bf16[128,640]{1,0:T(8,128)(2,1)S(1)}, u32[]{:S(2)}, u32[]{:S(2)}) collective-permute-start(bf16[128,640]{1,0:T(8,128)(2,1)S(1)} %slice.8), channel_id=1, source_target_pairs={{0,2},{1,3},{2,8},{3,9},{4,6},{5,7},{6,12},{7,13},{8,10},{9,11},{1... | collective-permute-start | bytes 491528 | tf_op jit(solution)/shard_map/ppermute | solution.py:36
  58.0 19.6 %collective-permute-done.7.ts_ref = bf16[128,640]{1,0:T(8,128)(2,1)S(1)} collective-permute-done((bf16[128,640]{1,0:T(8,128)(2,1)S(1)}, bf16[128,640]{1,0:T(8,128)(2,1)S(1)}, u32[]{:S(2)}, u32[]{:S(2)}) %collective-permute-start.7) | collective-permute-done | bytes 163872 | tf_op jit(solution)/shard_map/ppermute | solution.py:36
  77.6 0.0 copy-start.5
  77.6 34.7 %collective-permute-done.5.r_ref = bf16[512,640]{1,0:T(8,128)(2,1)S(1)} collective-permute-done((bf16[512,640]{1,0:T(8,128)(2,1)S(1)}, bf16[512,640]{1,0:T(8,128)(2,1)S(1)}, u32[]{:S(2)}, u32[]{:S(2)}) %collective-permute-start.5) | collective-permute-done | bytes 655392 | tf_op jit(solution)/shard_map/ppermute | solution.py:31
  112.2 0.0 copy-start.2
  112.2 0.0 collective-permute-done.6.a_ref
  112.2 0.0 copy-start.3
  112.2 3.1 %collective-permute-start.8 = (bf16[512,640]{1,0:T(8,128)(2,1)S(1)}, bf16[512,640]{1,0:T(8,128)(2,1)S(1)}, u32[]{:S(2)}, u32[]{:S(2)}) collective-permute-start(bf16[512,640]{1,0:T(8,128)(2,1)S(1)} %collective-permute-done.5.r_ref), channel_id=1, source_target_pairs={{0,1},{1,2},{2,3},{3,0},{8,9},{9,10},{10,11},{11,8},{16,17},{17,18... | collective-permute-start | bytes 1966088 | tf_op jit(solution)/shard_map/ppermute | solution.py:31
  115.4 4.4 %collective-permute-start.9 = (bf16[128,640]{1,0:T(8,128)(2,1)S(1)}, bf16[128,640]{1,0:T(8,128)(2,1)S(1)}, u32[]{:S(2)}, u32[]{:S(2)}) collective-permute-start(bf16[128,640]{1,0:T(8,128)(2,1)S(1)} %slice.9), channel_id=1, source_target_pairs={{0,2},{1,3},{2,0},{3,1},{8,10},{9,11},{10,8},{11,9},{16,18},{17,19... | collective-permute-start | bytes 491528 | tf_op jit(solution)/shard_map/ppermute | solution.py:31
  119.7 23.7 %collective-permute-done.9.tr_ref = bf16[128,640]{1,0:T(8,128)(2,1)S(1)} collective-permute-done((bf16[128,640]{1,0:T(8,128)(2,1)S(1)}, bf16[128,640]{1,0:T(8,128)(2,1)S(1)}, u32[]{:S(2)}, u32[]{:S(2)}) %collective-permute-start.9) | collective-permute-done | bytes 163872 | tf_op jit(solution)/shard_map/ppermute | solution.py:31
  143.4 0.0 copy-start.6
  143.4 5.9 %collective-permute-done.8.b_ref = bf16[512,640]{1,0:T(8,128)(2,1)S(1)} collective-permute-done((bf16[512,640]{1,0:T(8,128)(2,1)S(1)}, bf16[512,640]{1,0:T(8,128)(2,1)S(1)}, u32[]{:S(2)}, u32[]{:S(2)}) %collective-permute-start.8) | collective-permute-done | bytes 655392 | tf_op jit(solution)/shard_map/ppermute | solution.py:31
  149.3 0.0 copy-start.4
  149.3 2.0 %all-gather.3.cloned.1.call-done = bf16[10240,640]{1,0:T(8,128)(2,1)} async-done(((bf16[320,640]{1,0:T(8,128)(2,1)}), bf16[10240,640]{1,0:T(8,128)(2,1)}) %all-gather.3.cloned.1.call-update) | async-done | bytes 13107216 | tf_op jit(solution)/shard_map/all_gather | solution.py:187
  151.3 0.0 copy-done.5
  151.3 0.0 copy-done.2
  151.3 0.0 copy-done.3
  151.3 0.0 copy-done.6
  151.3 0.0 copy-done.4
  151.3 28.4 %shard_map.64 = bf16[512,640]{1,0:T(8,128)(2,1)} custom-call(s32[5]{0:T(128)} %stack.39.where, bf16[512,640]{1,0:T(8,128)(2,1)} %s_ref, bf16[512,640]{1,0:T(8,128)(2,1)} %copy-done.3, bf16[512,640]{1,0:T(8,128)(2,1)} %copy-done.2, bf16[512,640]{1,0:T(8,128)(2,1)} %copy-done.4, bf16[128,640]{1,0:T(8,128)(2,1)} %copy-done.5, bf16[128,640]{1,0:T(8,128)(2,1)} %copy-done.6, ...), custom_call_target="tpu_custom_call" | custom-call | flops 15000000512 | bytes 16000000 | tf_op jit(solution)/shard_map/pallas_call | solution.py:141
  (10 shorter events, 0.1 us)
Async XLA Ops:
  6.5 37.4 %copy-start = (bf16[512,640]{1,0:T(8,128)(2,1)S(1)}, bf16[512,640]{1,0:T(8,128)(2,1)}, u32[]{:S(2)}) copy-start(bf16[512,640]{1,0:T(8,128)(2,1)} %s_ref) | copy-start | bytes 1966084
  6.5 144.8 %all-gather.3.cloned.1.call-start = ((), (), s32[]{:S(2)}) async-start(), calls=%async_computation | async-start | bytes 13516800 | tf_op jit(solution)/shard_map/all_gather | solution.py:187
  7.5 9.3 %collective-permute-start.1 = (bf16[40,640]{1,0:T(8,128)(2,1)S(1)}, bf16[40,640]{1,0:T(8,128)(2,1)S(1)}, u32[]{:S(2)}, u32[]{:S(2)}) collective-permute-start(bf16[40,640]{1,0:T(8,128)(2,1)S(1)} %bitcast_select_fusion), channel_id=1, source_target_pairs={{0,452},{1,453},{2,454},{3,455},{8,460},{9,461},{10,462},{11,463},... | collective-permute-start | bytes 153608 | tf_op jit(solution)/shard_map/ppermute | solution.py:31
  9.4 13.6 %collective-permute-start = (bf16[40,640]{1,0:T(8,128)(2,1)S(1)}, bf16[40,640]{1,0:T(8,128)(2,1)S(1)}, u32[]{:S(2)}, u32[]{:S(2)}) collective-permute-start(bf16[40,640]{1,0:T(8,128)(2,1)S(1)} %bitcast_select_fusion), channel_id=1, source_target_pairs={{0,64},{1,65},{2,66},{3,67},{8,72},{9,73},{10,74},{11,75},{16,80},... | collective-permute-start | bytes 153608 | tf_op jit(solution)/shard_map/ppermute | solution.py:31
  14.2 29.0 %collective-permute-start.4 = (bf16[512,640]{1,0:T(8,128)(2,1)}, bf16[512,640]{1,0:T(8,128)(2,1)S(1)}, u32[]{:S(2)}, u32[]{:S(2)}) collective-permute-start(bf16[512,640]{1,0:T(8,128)(2,1)} %s_ref), channel_id=1, source_target_pairs={{4,12},{5,13},{6,14},{7,15},{12,20},{13,21},{14,22},{15,23},{20,28... | collective-permute-start | bytes 1966088 | tf_op jit(solution)/shard_map/ppermute | solution.py:172
  16.8 26.4 %collective-permute-start.3 = (bf16[80,640]{1,0:T(8,128)(2,1)S(1)}, bf16[80,640]{1,0:T(8,128)(2,1)S(1)}, u32[]{:S(2)}, u32[]{:S(2)}) collective-permute-start(bf16[80,640]{1,0:T(8,128)(2,1)S(1)} %pad_maximum_fusion.1), channel_id=1, source_target_pairs={{0,192},{1,193},{2,194},{3,195},{8,200},{9,201},{10,202},{11,203},... | collective-permute-start | bytes 307208 | tf_op jit(solution)/shard_map/ppermute | solution.py:31
  23.1 20.1 %collective-permute-start.2 = (bf16[120,640]{1,0:T(8,128)(2,1)S(1)}, bf16[120,640]{1,0:T(8,128)(2,1)S(1)}, u32[]{:S(2)}, u32[]{:S(2)}) collective-permute-start(bf16[120,640]{1,0:T(8,128)(2,1)S(1)} %pad_maximum_fusion), channel_id=1, source_target_pairs={{0,324},{1,325},{2,326},{3,327},{8,332},{9,333},{10,334},{11,335},... | collective-permute-start | bytes 460808 | tf_op jit(solution)/shard_map/ppermute | solution.py:31
  43.2 0.8 copy-start.1
  44.1 68.2 %collective-permute-start.5 = (bf16[512,640]{1,0:T(8,128)(2,1)S(1)}, bf16[512,640]{1,0:T(8,128)(2,1)S(1)}, u32[]{:S(2)}, u32[]{:S(2)}) collective-permute-start(bf16[512,640]{1,0:T(8,128)(2,1)S(1)} %broadcast_select_fusion), channel_id=1, source_target_pairs={{0,4},{1,5},{2,6},{3,7},{8,12},{9,13},{10,14},{11,15},{16,20},{17,... | collective-permute-start | bytes 1966088 | tf_op jit(solution)/shard_map/ppermute | solution.py:31
  50.5 61.7 %collective-permute-start.6 = (bf16[512,640]{1,0:T(8,128)(2,1)S(1)}, bf16[512,640]{1,0:T(8,128)(2,1)S(1)}, u32[]{:S(2)}, u32[]{:S(2)}) collective-permute-start(bf16[512,640]{1,0:T(8,128)(2,1)S(1)} %copy-done), channel_id=1, source_target_pairs={{0,1},{1,2},{2,3},{3,8},{4,5},{5,6},{6,7},{7,12},{8,9},{9,10},{10,... | collective-permute-start | bytes 1966088 | tf_op jit(solution)/shard_map/ppermute | solution.py:36
  53.6 23.9 %collective-permute-start.7 = (bf16[128,640]{1,0:T(8,128)(2,1)S(1)}, bf16[128,640]{1,0:T(8,128)(2,1)S(1)}, u32[]{:S(2)}, u32[]{:S(2)}) collective-permute-start(bf16[128,640]{1,0:T(8,128)(2,1)S(1)} %slice.8), channel_id=1, source_target_pairs={{0,2},{1,3},{2,8},{3,9},{4,6},{5,7},{6,12},{7,13},{8,10},{9,11},{1... | collective-permute-start | bytes 491528 | tf_op jit(solution)/shard_map/ppermute | solution.py:36
  77.6 73.8 %copy-start.5 = (bf16[128,640]{1,0:T(8,128)(2,1)}, bf16[128,640]{1,0:T(8,128)(2,1)S(1)}, u32[]{:S(2)}) copy-start(bf16[128,640]{1,0:T(8,128)(2,1)S(1)} %collective-permute-done.7.ts_ref) | copy-start | bytes 491524
  112.2 39.1 %copy-start.2 = (bf16[512,640]{1,0:T(8,128)(2,1)}, bf16[512,640]{1,0:T(8,128)(2,1)S(1)}, u32[]{:S(2)}) copy-start(bf16[512,640]{1,0:T(8,128)(2,1)S(1)} %collective-permute-done.5.r_ref) | copy-start | bytes 1966084
  112.2 39.1 %copy-start.3 = (bf16[512,640]{1,0:T(8,128)(2,1)}, bf16[512,640]{1,0:T(8,128)(2,1)S(1)}, u32[]{:S(2)}) copy-start(bf16[512,640]{1,0:T(8,128)(2,1)S(1)} %collective-permute-done.6.a_ref) | copy-start | bytes 1966084
  112.2 37.0 %collective-permute-start.8 = (bf16[512,640]{1,0:T(8,128)(2,1)S(1)}, bf16[512,640]{1,0:T(8,128)(2,1)S(1)}, u32[]{:S(2)}, u32[]{:S(2)}) collective-permute-start(bf16[512,640]{1,0:T(8,128)(2,1)S(1)} %collective-permute-done.5.r_ref), channel_id=1, source_target_pairs={{0,1},{1,2},{2,3},{3,0},{8,9},{9,10},{10,11},{11,8},{16,17},{17,18... | collective-permute-start | bytes 1966088 | tf_op jit(solution)/shard_map/ppermute | solution.py:31
  115.4 28.0 %collective-permute-start.9 = (bf16[128,640]{1,0:T(8,128)(2,1)S(1)}, bf16[128,640]{1,0:T(8,128)(2,1)S(1)}, u32[]{:S(2)}, u32[]{:S(2)}) collective-permute-start(bf16[128,640]{1,0:T(8,128)(2,1)S(1)} %slice.9), channel_id=1, source_target_pairs={{0,2},{1,3},{2,0},{3,1},{8,10},{9,11},{10,8},{11,9},{16,18},{17,19... | collective-permute-start | bytes 491528 | tf_op jit(solution)/shard_map/ppermute | solution.py:31
  143.4 7.9 %copy-start.6 = (bf16[128,640]{1,0:T(8,128)(2,1)}, bf16[128,640]{1,0:T(8,128)(2,1)S(1)}, u32[]{:S(2)}) copy-start(bf16[128,640]{1,0:T(8,128)(2,1)S(1)} %collective-permute-done.9.tr_ref) | copy-start | bytes 491524
  149.3 2.1 %copy-start.4 = (bf16[512,640]{1,0:T(8,128)(2,1)}, bf16[512,640]{1,0:T(8,128)(2,1)S(1)}, u32[]{:S(2)}) copy-start(bf16[512,640]{1,0:T(8,128)(2,1)S(1)} %collective-permute-done.8.b_ref) | copy-start | bytes 1966084
Sparse Core Ops, SparseCore 0:
  44.1 107.1 all-gather.2

commit v3 on v2

--- a/solution.py
+++ b/solution.py
@@ -72,16 +72,14 @@
         pltpu.make_async_copy(mix.at[layer], mix.at[layer], sems.at[3 + layer]).wait()
 
     def bring(ref, slot, tail_slot):
-        exact = jnp.dot(ref[...], perm_ref[...], preferred_element_type=jnp.float32)
-        x0[slot] = exact.astype(jnp.bfloat16)
-        unit = normed(exact)
+        x0[slot] = ref[...]
+        unit = normed(ref[...].astype(jnp.float32))
         u1[slot, TAIL:] = unit
         if tail_slot is not None:
             u1[tail_slot, :TAIL] = unit[BLOCK - TAIL :]
 
     def bring_tail(ref, slot):
-        exact = jnp.dot(ref[...], perm_ref[...], preferred_element_type=jnp.float32)
-        u1[slot, :TAIL] = normed(exact)
+        u1[slot, :TAIL] = normed(ref[...].astype(jnp.float32))
 
     a_slot = jnp.where(x == 0, 0, 2)
     t_slot = jnp.where(x < 2, 0, 2)
@@ -182,7 +180,7 @@
     channel = (shard * 2 + k // 320) * 40 + k % 40
     perm = (k[:, None] == channel[None, :]).astype(jnp.bfloat16)
     where = jnp.stack([x, block >= 5, block >= 4, block >= 1, block >= 0]).astype(jnp.int32)
-    near, own, stepped, perm, where = lax.optimization_barrier((near, own, stepped, perm, where))
+    near, own, stepped = lax.optimization_barrier((near, own, stepped))
 
     weights = lax.all_gather(near, ("core", "y", "x"))
     far = permuted(
@@ -190,10 +188,16 @@
     )
     beside = shifted(own, lambda b: b + 1 if b % 4 < 3 else b + 5)
     own_tail = shifted(own[BLOCK - TAIL :], lambda b: b + 2 if b % 4 < 2 else b + 6)
-    far, beside, own_tail = lax.optimization_barrier((far, beside, own_tail))
+    far, beside, own_tail, perm = lax.optimization_barrier((far, beside, own_tail, perm))
+
+    def reordered(rows):
+        return jnp.dot(rows, perm, preferred_element_type=jnp.float32).astype(jnp.bfloat16)
+
+    far = reordered(far)
     far_beside = permuted(far, lambda z, c, yy, xx: (z, c, yy, xx + 1))
     far_tail = permuted(far[BLOCK - TAIL :], lambda z, c, yy, xx: (z, c, yy, xx + 2))
 
+    own, beside, own_tail = reordered(own), reordered(beside), reordered(own_tail)
     rows_in = (own, beside, far, far_beside, own_tail, far_tail)
     return block_output(where, rows_in, perm, conv_bias, weights)
 

time: 187 us -> 185 us (0.989)
  waiting for transfers between devices: 103 us -> 90.5 us
  starting transfers between devices: 37.9 us -> 45.9 us
  matrix products: 0 us -> 4.88 us
    ppermute x7, waiting for transfers between devices: 81.4 us -> 70 us  [permuted(): return lax.ppermute(value, AXES, pairs)]
    ppermute x7, starting transfers between devices: 29.7 us -> 37.7 us  [permuted(): return lax.ppermute(value, AXES, pairs)]
    dot_general x0 -> x4, matrix products: none -> 4.88 us  [reordered(): jnp.dot(rows, perm, preferred_element_type=jnp.float32).astype(jnp.bfloat16)]
  transfers between devices with their start and end apart: 11 -> 11, of which waited for: 6 -> 6; matrix products, arithmetic and copies ran while one was open for 1% -> 3% of each run, Pallas kernels for 0% -> 0%
where the time goes in v3:
time: 185 us
  waiting for transfers between devices  90.5 us (49%)
  starting transfers between devices  45.9 us (25%)
  Pallas kernels  26.7 us (14%)
  between operations  13.7 us (7%)
  matrix products  4.88 us (3%)
    ppermute x7, waiting for transfers between devices, permuted(): return lax.ppermute(value, AXES, pairs)  70 us
    ppermute x7, starting transfers between devices, permuted(): return lax.ppermute(value, AXES, pairs)  37.7 us
    pallas_call x1, Pallas kernels, block_output(): pl.pallas_call(kernel, out_shape=jax.ShapeDtypeStruct((BLOCK, D), jnp.bfl...  26.7 us
    ppermute x2, waiting for transfers between devices, shifted(): return lax.ppermute(value, AXES, [(a, b) for a, b in pairs if b < DEVICES])  18.5 us
    ppermute x2, starting transfers between devices, shifted(): return lax.ppermute(value, AXES, [(a, b) for a, b in pairs if b < DEVICES])  7.48 us
    dot_general x4, matrix products, reordered(): jnp.dot(rows, perm, preferred_element_type=jnp.float32).astype(jnp.bfloat16)  4.88 us
  transfers between devices with their start and end apart: 11, of which 6 were waited for; matrix products, arithmetic and copies ran while one was open for 3% of the time, Pallas kernels for 0%

profile of v3, /device:TPU:121, one launch (start us, length us, event | category | flops | bytes accessed | tf_op | source)
XLA Modules:
  0.0 184.5 jit_solution(13429811120737627472)
XLA Ops:
  6.5 0.0 copy-start.1
  6.5 0.0 all-gather.3.cloned.1.call-start
  6.5 0.9 bitcast_select_fusion
  7.5 1.9 %collective-permute-start.1 = (bf16[40,640]{1,0:T(8,128)(2,1)S(1)}, bf16[40,640]{1,0:T(8,128)(2,1)S(1)}, u32[]{:S(2)}, u32[]{:S(2)}) collective-permute-start(bf16[40,640]{1,0:T(8,128)(2,1)S(1)} %bitcast_select_fusion), channel_id=1, source_target_pairs={{0,452},{1,453},{2,454},{3,455},{8,460},{9,461},{10,462},{11,463},... | collective-permute-start | bytes 153608 | tf_op jit(solution)/shard_map/ppermute | solution.py:31
  9.4 4.8 %collective-permute-start = (bf16[40,640]{1,0:T(8,128)(2,1)S(1)}, bf16[40,640]{1,0:T(8,128)(2,1)S(1)}, u32[]{:S(2)}, u32[]{:S(2)}) collective-permute-start(bf16[40,640]{1,0:T(8,128)(2,1)S(1)} %bitcast_select_fusion), channel_id=1, source_target_pairs={{0,64},{1,65},{2,66},{3,67},{8,72},{9,73},{10,74},{11,75},{16,80},... | collective-permute-start | bytes 153608 | tf_op jit(solution)/shard_map/ppermute | solution.py:31
  14.2 0.7 collective-permute-start.4
  14.9 0.0 collective-permute-done.1
  14.9 6.3 %collective-permute-start.3 = (bf16[80,640]{1,0:T(8,128)(2,1)S(1)}, bf16[80,640]{1,0:T(8,128)(2,1)S(1)}, u32[]{:S(2)}, u32[]{:S(2)}) collective-permute-start(bf16[80,640]{1,0:T(8,128)(2,1)S(1)} %pad_maximum_fusion.1), channel_id=1, source_target_pairs={{0,192},{1,193},{2,194},{3,195},{8,200},{9,201},{10,202},{11,203},... | collective-permute-start | bytes 307208 | tf_op jit(solution)/shard_map/ppermute | solution.py:31
  21.2 0.0 collective-permute-done
  21.2 4.3 %collective-permute-start.2 = (bf16[120,640]{1,0:T(8,128)(2,1)S(1)}, bf16[120,640]{1,0:T(8,128)(2,1)S(1)}, u32[]{:S(2)}, u32[]{:S(2)}) collective-permute-start(bf16[120,640]{1,0:T(8,128)(2,1)S(1)} %pad_maximum_fusion), channel_id=1, source_target_pairs={{0,324},{1,325},{2,326},{3,327},{8,332},{9,333},{10,334},{11,335},... | collective-permute-start | bytes 460808 | tf_op jit(solution)/shard_map/ppermute | solution.py:31
  25.6 15.7 %collective-permute-done.2 = bf16[120,640]{1,0:T(8,128)(2,1)S(1)} collective-permute-done((bf16[120,640]{1,0:T(8,128)(2,1)S(1)}, bf16[120,640]{1,0:T(8,128)(2,1)S(1)}, u32[]{:S(2)}, u32[]{:S(2)}) %collective-permute-start.2) | collective-permute-done | bytes 153632 | tf_op jit(solution)/shard_map/ppermute | solution.py:31
  41.3 0.0 collective-permute-done.3
  41.4 0.0 copy-start.2
  41.4 0.0 collective-permute-done.4
  41.4 0.7 copy-done.2
  42.1 0.0 all-gather.3.cloned.1.call-update
  42.1 0.0 copy-done.1
  42.1 0.1 broadcast_select_fusion
  42.2 7.4 %collective-permute-start.5 = (bf16[512,640]{1,0:T(8,128)(2,1)S(1)}, bf16[512,640]{1,0:T(8,128)(2,1)S(1)}, u32[]{:S(2)}, u32[]{:S(2)}) collective-permute-start(bf16[512,640]{1,0:T(8,128)(2,1)S(1)} %broadcast_select_fusion), channel_id=1, source_target_pairs={{0,4},{1,5},{2,6},{3,7},{8,12},{9,13},{10,14},{11,15},{16,20},{17,... | collective-permute-start | bytes 1966088 | tf_op jit(solution)/shard_map/ppermute | solution.py:31
  49.6 3.1 %collective-permute-start.6 = (bf16[512,640]{1,0:T(8,128)(2,1)S(1)}, bf16[512,640]{1,0:T(8,128)(2,1)S(1)}, u32[]{:S(2)}, u32[]{:S(2)}) collective-permute-start(bf16[512,640]{1,0:T(8,128)(2,1)S(1)} %copy-done.1), channel_id=1, source_target_pairs={{0,1},{1,2},{2,3},{3,8},{4,5},{5,6},{6,7},{7,12},{8,9},{9,10},{10,... | collective-permute-start | bytes 1966088 | tf_op jit(solution)/shard_map/ppermute | solution.py:36
  52.8 0.6 stack.39.where
  53.4 0.1 compare_reduce_fusion
  53.5 0.1 fusion.12
  53.6 4.4 %collective-permute-start.7 = (bf16[128,640]{1,0:T(8,128)(2,1)S(1)}, bf16[128,640]{1,0:T(8,128)(2,1)S(1)}, u32[]{:S(2)}, u32[]{:S(2)}) collective-permute-start(bf16[128,640]{1,0:T(8,128)(2,1)S(1)} %slice.8), channel_id=1, source_target_pairs={{0,2},{1,3},{2,8},{3,9},{4,6},{5,7},{6,12},{7,13},{8,10},{9,11},{1... | collective-permute-start | bytes 491528 | tf_op jit(solution)/shard_map/ppermute | solution.py:36
  57.9 0.2 fusion.perm_ref
  58.2 0.0 copy-start
  58.2 18.5 %collective-permute-done.7 = bf16[128,640]{1,0:T(8,128)(2,1)S(1)} collective-permute-done((bf16[128,640]{1,0:T(8,128)(2,1)S(1)}, bf16[128,640]{1,0:T(8,128)(2,1)S(1)}, u32[]{:S(2)}, u32[]{:S(2)}) %collective-permute-start.7) | collective-permute-done | bytes 163872 | tf_op jit(solution)/shard_map/ppermute | solution.py:36
  76.7 30.3 %collective-permute-done.5 = bf16[512,640]{1,0:T(8,128)(2,1)S(1)} collective-permute-done((bf16[512,640]{1,0:T(8,128)(2,1)S(1)}, bf16[512,640]{1,0:T(8,128)(2,1)S(1)}, u32[]{:S(2)}, u32[]{:S(2)}) %collective-permute-start.5) | collective-permute-done | bytes 655392 | tf_op jit(solution)/shard_map/ppermute | solution.py:31
  107.0 0.0 collective-permute-done.6
  107.0 0.7 convolution_convert_fusion.r_ref
  107.8 0.0 copy-start.3
  107.8 3.1 %collective-permute-start.8 = (bf16[512,640]{1,0:T(8,128)(2,1)S(1)}, bf16[512,640]{1,0:T(8,128)(2,1)S(1)}, u32[]{:S(2)}, u32[]{:S(2)}) collective-permute-start(bf16[512,640]{1,0:T(8,128)(2,1)S(1)} %convolution_convert_fusion.r_ref), channel_id=1, source_target_pairs={{0,1},{1,2},{2,3},{3,0},{8,9},{9,10},{10,11},{11,8},{16,17},{17,18... | collective-permute-start | bytes 1966088 | tf_op jit(solution)/shard_map/ppermute | solution.py:31
  110.9 1.6 convolution_convert_fusion.2.s_ref
  112.5 9.9 %collective-permute-start.9 = (bf16[128,640]{1,0:T(8,128)(2,1)S(1)}, bf16[128,640]{1,0:T(8,128)(2,1)S(1)}, u32[]{:S(2)}, u32[]{:S(2)}) collective-permute-start(bf16[128,640]{1,0:T(8,128)(2,1)S(1)} %slice.19), channel_id=1, source_target_pairs={{0,2},{1,3},{2,0},{3,1},{8,10},{9,11},{10,8},{11,9},{16,18},{17,19... | collective-permute-start | bytes 491528 | tf_op jit(solution)/shard_map/ppermute | solution.py:31
  122.4 1.6 convolution_convert_fusion.1.a_ref
  124.0 0.0 copy-done
  124.0 0.0 copy-done.3
  124.0 1.0 convolution_convert_fusion.3.ts_ref
  125.0 17.1 %collective-permute-done.9.tr_ref = bf16[128,640]{1,0:T(8,128)(2,1)S(1)} collective-permute-done((bf16[128,640]{1,0:T(8,128)(2,1)S(1)}, bf16[128,640]{1,0:T(8,128)(2,1)S(1)}, u32[]{:S(2)}, u32[]{:S(2)}) %collective-permute-start.9) | collective-permute-done | bytes 163872 | tf_op jit(solution)/shard_map/ppermute | solution.py:31
  142.1 0.0 copy-start.5
  142.1 6.9 %collective-permute-done.8.b_ref = bf16[512,640]{1,0:T(8,128)(2,1)S(1)} collective-permute-done((bf16[512,640]{1,0:T(8,128)(2,1)S(1)}, bf16[512,640]{1,0:T(8,128)(2,1)S(1)}, u32[]{:S(2)}, u32[]{:S(2)}) %collective-permute-start.8) | collective-permute-done | bytes 655392 | tf_op jit(solution)/shard_map/ppermute | solution.py:31
  149.0 0.0 copy-start.4
  149.0 1.9 %all-gather.3.cloned.1.call-done = bf16[10240,640]{1,0:T(8,128)(2,1)} async-done(((bf16[320,640]{1,0:T(8,128)(2,1)}), bf16[10240,640]{1,0:T(8,128)(2,1)}) %all-gather.3.cloned.1.call-update) | async-done | bytes 13107216 | tf_op jit(solution)/shard_map/all_gather | solution.py:185
  150.9 0.0 copy-done.5
  150.9 0.0 copy-done.4
  150.9 26.7 %shard_map.64 = bf16[512,640]{1,0:T(8,128)(2,1)} custom-call(s32[5]{0:T(128)} %stack.39.where, bf16[512,640]{1,0:T(8,128)(2,1)} %convolution_convert_fusion.2.s_ref, bf16[512,640]{1,0:T(8,128)(2,1)} %convolution_convert_fusion.1.a_ref, bf16[512,640]{1,0:T(8,128)(2,1)} %copy-done.3, bf16[512,640]{1,0:T(8,128)(2,1)} %copy-done.4, ...), custom_call_target="tpu_custom_call" | custom-call | flops 15000000512 | bytes 16000000 | tf_op jit(solution)/shard_map/pallas_call | solution.py:139
  (10 shorter events, 0.1 us)
Async XLA Ops:
  6.5 35.6 %copy-start.1 = (bf16[512,640]{1,0:T(8,128)(2,1)S(1)}, bf16[512,640]{1,0:T(8,128)(2,1)}, u32[]{:S(2)}) copy-start(bf16[512,640]{1,0:T(8,128)(2,1)} %param.6) | copy-start | bytes 1966084
  6.5 144.4 %all-gather.3.cloned.1.call-start = ((), (), s32[]{:S(2)}) async-start(), calls=%async_computation | async-start | bytes 13516800 | tf_op jit(solution)/shard_map/all_gather | solution.py:185
  7.5 7.4 %collective-permute-start.1 = (bf16[40,640]{1,0:T(8,128)(2,1)S(1)}, bf16[40,640]{1,0:T(8,128)(2,1)S(1)}, u32[]{:S(2)}, u32[]{:S(2)}) collective-permute-start(bf16[40,640]{1,0:T(8,128)(2,1)S(1)} %bitcast_select_fusion), channel_id=1, source_target_pairs={{0,452},{1,453},{2,454},{3,455},{8,460},{9,461},{10,462},{11,463},... | collective-permute-start | bytes 153608 | tf_op jit(solution)/shard_map/ppermute | solution.py:31
  9.4 11.8 %collective-permute-start = (bf16[40,640]{1,0:T(8,128)(2,1)S(1)}, bf16[40,640]{1,0:T(8,128)(2,1)S(1)}, u32[]{:S(2)}, u32[]{:S(2)}) collective-permute-start(bf16[40,640]{1,0:T(8,128)(2,1)S(1)} %bitcast_select_fusion), channel_id=1, source_target_pairs={{0,64},{1,65},{2,66},{3,67},{8,72},{9,73},{10,74},{11,75},{16,80},... | collective-permute-start | bytes 153608 | tf_op jit(solution)/shard_map/ppermute | solution.py:31
  14.2 27.2 %collective-permute-start.4 = (bf16[512,640]{1,0:T(8,128)(2,1)}, bf16[512,640]{1,0:T(8,128)(2,1)S(1)}, u32[]{:S(2)}, u32[]{:S(2)}) collective-permute-start(bf16[512,640]{1,0:T(8,128)(2,1)} %param.6), channel_id=1, source_target_pairs={{4,12},{5,13},{6,14},{7,15},{12,20},{13,21},{14,22},{15,23},{20,28... | collective-permute-start | bytes 1966088 | tf_op jit(solution)/shard_map/ppermute | solution.py:170
  14.9 26.4 %collective-permute-start.3 = (bf16[80,640]{1,0:T(8,128)(2,1)S(1)}, bf16[80,640]{1,0:T(8,128)(2,1)S(1)}, u32[]{:S(2)}, u32[]{:S(2)}) collective-permute-start(bf16[80,640]{1,0:T(8,128)(2,1)S(1)} %pad_maximum_fusion.1), channel_id=1, source_target_pairs={{0,192},{1,193},{2,194},{3,195},{8,200},{9,201},{10,202},{11,203},... | collective-permute-start | bytes 307208 | tf_op jit(solution)/shard_map/ppermute | solution.py:31
  21.2 20.1 %collective-permute-start.2 = (bf16[120,640]{1,0:T(8,128)(2,1)S(1)}, bf16[120,640]{1,0:T(8,128)(2,1)S(1)}, u32[]{:S(2)}, u32[]{:S(2)}) collective-permute-start(bf16[120,640]{1,0:T(8,128)(2,1)S(1)} %pad_maximum_fusion), channel_id=1, source_target_pairs={{0,324},{1,325},{2,326},{3,327},{8,332},{9,333},{10,334},{11,335},... | collective-permute-start | bytes 460808 | tf_op jit(solution)/shard_map/ppermute | solution.py:31
  41.4 0.8 copy-start.2
  42.2 64.8 %collective-permute-start.5 = (bf16[512,640]{1,0:T(8,128)(2,1)S(1)}, bf16[512,640]{1,0:T(8,128)(2,1)S(1)}, u32[]{:S(2)}, u32[]{:S(2)}) collective-permute-start(bf16[512,640]{1,0:T(8,128)(2,1)S(1)} %broadcast_select_fusion), channel_id=1, source_target_pairs={{0,4},{1,5},{2,6},{3,7},{8,12},{9,13},{10,14},{11,15},{16,20},{17,... | collective-permute-start | bytes 1966088 | tf_op jit(solution)/shard_map/ppermute | solution.py:31
  49.6 57.4 %collective-permute-start.6 = (bf16[512,640]{1,0:T(8,128)(2,1)S(1)}, bf16[512,640]{1,0:T(8,128)(2,1)S(1)}, u32[]{:S(2)}, u32[]{:S(2)}) collective-permute-start(bf16[512,640]{1,0:T(8,128)(2,1)S(1)} %copy-done.1), channel_id=1, source_target_pairs={{0,1},{1,2},{2,3},{3,8},{4,5},{5,6},{6,7},{7,12},{8,9},{9,10},{10,... | collective-permute-start | bytes 1966088 | tf_op jit(solution)/shard_map/ppermute | solution.py:36
  53.6 23.2 %collective-permute-start.7 = (bf16[128,640]{1,0:T(8,128)(2,1)S(1)}, bf16[128,640]{1,0:T(8,128)(2,1)S(1)}, u32[]{:S(2)}, u32[]{:S(2)}) collective-permute-start(bf16[128,640]{1,0:T(8,128)(2,1)S(1)} %slice.8), channel_id=1, source_target_pairs={{0,2},{1,3},{2,8},{3,9},{4,6},{5,7},{6,12},{7,13},{8,10},{9,11},{1... | collective-permute-start | bytes 491528 | tf_op jit(solution)/shard_map/ppermute | solution.py:36
  58.2 65.8 %copy-start = (bf16[640,640]{1,0:T(8,128)(2,1)}, bf16[640,640]{1,0:T(8,128)(2,1)S(1)}, u32[]{:S(2)}) copy-start(bf16[640,640]{1,0:T(8,128)(2,1)S(1)} %fusion.perm_ref) | copy-start | bytes 2457604
  107.8 16.2 %copy-start.3 = (bf16[512,640]{1,0:T(8,128)(2,1)}, bf16[512,640]{1,0:T(8,128)(2,1)S(1)}, u32[]{:S(2)}) copy-start(bf16[512,640]{1,0:T(8,128)(2,1)S(1)} %convolution_convert_fusion.r_ref) | copy-start | bytes 1966084
  107.8 41.2 %collective-permute-start.8 = (bf16[512,640]{1,0:T(8,128)(2,1)S(1)}, bf16[512,640]{1,0:T(8,128)(2,1)S(1)}, u32[]{:S(2)}, u32[]{:S(2)}) collective-permute-start(bf16[512,640]{1,0:T(8,128)(2,1)S(1)} %convolution_convert_fusion.r_ref), channel_id=1, source_target_pairs={{0,1},{1,2},{2,3},{3,0},{8,9},{9,10},{10,11},{11,8},{16,17},{17,18... | collective-permute-start | bytes 1966088 | tf_op jit(solution)/shard_map/ppermute | solution.py:31
  112.5 29.6 %collective-permute-start.9 = (bf16[128,640]{1,0:T(8,128)(2,1)S(1)}, bf16[128,640]{1,0:T(8,128)(2,1)S(1)}, u32[]{:S(2)}, u32[]{:S(2)}) collective-permute-start(bf16[128,640]{1,0:T(8,128)(2,1)S(1)} %slice.19), channel_id=1, source_target_pairs={{0,2},{1,3},{2,0},{3,1},{8,10},{9,11},{10,8},{11,9},{16,18},{17,19... | collective-permute-start | bytes 491528 | tf_op jit(solution)/shard_map/ppermute | solution.py:31
  142.1 8.9 %copy-start.5 = (bf16[128,640]{1,0:T(8,128)(2,1)}, bf16[128,640]{1,0:T(8,128)(2,1)S(1)}, u32[]{:S(2)}) copy-start(bf16[128,640]{1,0:T(8,128)(2,1)S(1)} %collective-permute-done.9.tr_ref) | copy-start | bytes 491524
  149.0 1.9 %copy-start.4 = (bf16[512,640]{1,0:T(8,128)(2,1)}, bf16[512,640]{1,0:T(8,128)(2,1)S(1)}, u32[]{:S(2)}) copy-start(bf16[512,640]{1,0:T(8,128)(2,1)S(1)} %collective-permute-done.8.b_ref) | copy-start | bytes 1966084
Sparse Core Ops, SparseCore 0:
  42.3 108.6 all-gather.2

commit v4 on v3

--- a/solution.py
+++ b/solution.py
@@ -180,13 +180,13 @@
     channel = (shard * 2 + k // 320) * 40 + k % 40
     perm = (k[:, None] == channel[None, :]).astype(jnp.bfloat16)
     where = jnp.stack([x, block >= 5, block >= 4, block >= 1, block >= 0]).astype(jnp.int32)
-    near, own, stepped = lax.optimization_barrier((near, own, stepped))
+    beside = shifted(own, lambda b: b + 1 if b % 4 < 3 else b + 5)
+    near, own, stepped, beside = lax.optimization_barrier((near, own, stepped, beside))
 
     weights = lax.all_gather(near, ("core", "y", "x"))
     far = permuted(
         jnp.where(zh == 1, stepped, own), lambda z, c, yy, xx: (z + 8, c, yy, xx)
     )
-    beside = shifted(own, lambda b: b + 1 if b % 4 < 3 else b + 5)
     own_tail = shifted(own[BLOCK - TAIL :], lambda b: b + 2 if b % 4 < 2 else b + 6)
     far, beside, own_tail, perm = lax.optimization_barrier((far, beside, own_tail, perm))
 

time: 185 us -> 181 us (0.978)
  the two profiles are of different devices: /device:TPU:121 before, /device:TPU:33 now
where the time goes in v4:
time: 181 us
  waiting for transfers between devices  74 us (41%)
  starting transfers between devices  57.7 us (32%)
  Pallas kernels  26.7 us (15%)
  between operations  13.7 us (8%)
  matrix products  6.05 us (3%)
    ppermute x7, waiting for transfers between devices, permuted(): return lax.ppermute(value, AXES, pairs)  62.4 us
    ppermute x7, starting transfers between devices, permuted(): return lax.ppermute(value, AXES, pairs)  52 us
    pallas_call x1, Pallas kernels, block_output(): pl.pallas_call(kernel, out_shape=jax.ShapeDtypeStruct((BLOCK, D), jnp.bfl...  26.7 us
    ppermute x2, waiting for transfers between devices, shifted(): return lax.ppermute(value, AXES, [(a, b) for a, b in pairs if b < DEVICES])  11.6 us
    dot_general x4, matrix products, reordered(): jnp.dot(rows, perm, preferred_element_type=jnp.float32).astype(jnp.bfloat16)  6.05 us
    ppermute x2, starting transfers between devices, shifted(): return lax.ppermute(value, AXES, [(a, b) for a, b in pairs if b < DEVICES])  5.04 us
  transfers between devices with their start and end apart: 11, of which 5 were waited for; matrix products, arithmetic and copies ran while one was open for 4% of the time, Pallas kernels for 0%

profile of v4, /device:TPU:33, one launch (start us, length us, event | category | flops | bytes accessed | tf_op | source)
XLA Modules:
  0.0 181.0 jit_solution(1870392413973543515)
XLA Ops:
  6.5 0.0 copy-start.1
  6.5 0.0 all-gather.3.cloned.1.call-start
  6.5 0.9 bitcast_select_fusion
  7.5 1.9 %collective-permute-start.1 = (bf16[40,640]{1,0:T(8,128)(2,1)S(1)}, bf16[40,640]{1,0:T(8,128)(2,1)S(1)}, u32[]{:S(2)}, u32[]{:S(2)}) collective-permute-start(bf16[40,640]{1,0:T(8,128)(2,1)S(1)} %bitcast_select_fusion), channel_id=1, source_target_pairs={{0,452},{1,453},{2,454},{3,455},{8,460},{9,461},{10,462},{11,463},... | collective-permute-start | bytes 153608 | tf_op jit(solution)/shard_map/ppermute | solution.py:31
  9.4 3.5 %collective-permute-start = (bf16[40,640]{1,0:T(8,128)(2,1)S(1)}, bf16[40,640]{1,0:T(8,128)(2,1)S(1)}, u32[]{:S(2)}, u32[]{:S(2)}) collective-permute-start(bf16[40,640]{1,0:T(8,128)(2,1)S(1)} %bitcast_select_fusion), channel_id=1, source_target_pairs={{0,64},{1,65},{2,66},{3,67},{8,72},{9,73},{10,74},{11,75},{16,80},... | collective-permute-start | bytes 153608 | tf_op jit(solution)/shard_map/ppermute | solution.py:31
  13.0 0.7 collective-permute-start.4
  13.7 3.1 %collective-permute-start.5 = (bf16[512,640]{1,0:T(8,128)(2,1)}, bf16[512,640]{1,0:T(8,128)(2,1)S(1)}, u32[]{:S(2)}, u32[]{:S(2)}) collective-permute-start(bf16[512,640]{1,0:T(8,128)(2,1)} %param.6), channel_id=1, source_target_pairs={{0,1},{1,2},{2,3},{3,8},{4,5},{5,6},{6,7},{7,12},{8,9},{9,10},{10,... | collective-permute-start | bytes 1966088 | tf_op jit(solution)/shard_map/ppermute | solution.py:36
  16.8 0.0 collective-permute-done.1
  16.8 7.5 %collective-permute-start.3 = (bf16[80,640]{1,0:T(8,128)(2,1)S(1)}, bf16[80,640]{1,0:T(8,128)(2,1)S(1)}, u32[]{:S(2)}, u32[]{:S(2)}) collective-permute-start(bf16[80,640]{1,0:T(8,128)(2,1)S(1)} %pad_maximum_fusion.1), channel_id=1, source_target_pairs={{0,192},{1,193},{2,194},{3,195},{8,200},{9,201},{10,202},{11,203},... | collective-permute-start | bytes 307208 | tf_op jit(solution)/shard_map/ppermute | solution.py:31
  24.3 0.0 collective-permute-done
  24.3 7.9 %collective-permute-start.2 = (bf16[120,640]{1,0:T(8,128)(2,1)S(1)}, bf16[120,640]{1,0:T(8,128)(2,1)S(1)}, u32[]{:S(2)}, u32[]{:S(2)}) collective-permute-start(bf16[120,640]{1,0:T(8,128)(2,1)S(1)} %pad_maximum_fusion), channel_id=1, source_target_pairs={{0,324},{1,325},{2,326},{3,327},{8,332},{9,333},{10,334},{11,335},... | collective-permute-start | bytes 460808 | tf_op jit(solution)/shard_map/ppermute | solution.py:31
  32.3 2.4 %collective-permute-done.2 = bf16[120,640]{1,0:T(8,128)(2,1)S(1)} collective-permute-done((bf16[120,640]{1,0:T(8,128)(2,1)S(1)}, bf16[120,640]{1,0:T(8,128)(2,1)S(1)}, u32[]{:S(2)}, u32[]{:S(2)}) %collective-permute-start.2) | collective-permute-done | bytes 153632 | tf_op jit(solution)/shard_map/ppermute | solution.py:31
  34.7 0.0 collective-permute-done.3
  34.7 0.0 copy-start.2
  34.8 0.0 collective-permute-done.4
  34.8 0.0 collective-permute-done.5
  34.8 0.7 copy-done.2
  35.5 0.0 all-gather.3.cloned.1.call-update
  35.5 0.0 copy-done.1
  35.5 0.1 broadcast_select_fusion
  35.6 27.1 %collective-permute-start.6 = (bf16[512,640]{1,0:T(8,128)(2,1)S(1)}, bf16[512,640]{1,0:T(8,128)(2,1)}, u32[]{:S(2)}, u32[]{:S(2)}) collective-permute-start(bf16[512,640]{1,0:T(8,128)(2,1)S(1)} %broadcast_select_fusion), channel_id=1, source_target_pairs={{0,4},{1,5},{2,6},{3,7},{8,12},{9,13},{10,14},{11,15},{16,20},{17,... | collective-permute-start | bytes 1966088 | tf_op jit(solution)/shard_map/ppermute | solution.py:31
  62.8 0.6 stack.39.where
  63.4 0.1 compare_reduce_fusion
  63.4 0.1 fusion.12
  63.5 1.9 %collective-permute-start.7 = (bf16[128,640]{1,0:T(8,128)(2,1)S(1)}, bf16[128,640]{1,0:T(8,128)(2,1)S(1)}, u32[]{:S(2)}, u32[]{:S(2)}) collective-permute-start(bf16[128,640]{1,0:T(8,128)(2,1)S(1)} %slice.8), channel_id=1, source_target_pairs={{0,2},{1,3},{2,8},{3,9},{4,6},{5,7},{6,12},{7,13},{8,10},{9,11},{1... | collective-permute-start | bytes 491528 | tf_op jit(solution)/shard_map/ppermute | solution.py:36
  65.5 0.2 fusion.perm_ref
  65.7 0.0 copy-start
  65.7 11.6 %collective-permute-done.7 = bf16[128,640]{1,0:T(8,128)(2,1)S(1)} collective-permute-done((bf16[128,640]{1,0:T(8,128)(2,1)S(1)}, bf16[128,640]{1,0:T(8,128)(2,1)S(1)}, u32[]{:S(2)}, u32[]{:S(2)}) %collective-permute-start.7) | collective-permute-done | bytes 163872 | tf_op jit(solution)/shard_map/ppermute | solution.py:36
  77.3 38.2 %collective-permute-done.6 = bf16[512,640]{1,0:T(8,128)(2,1)} collective-permute-done((bf16[512,640]{1,0:T(8,128)(2,1)S(1)}, bf16[512,640]{1,0:T(8,128)(2,1)}, u32[]{:S(2)}, u32[]{:S(2)}) %collective-permute-start.6) | collective-permute-done | bytes 655392 | tf_op jit(solution)/shard_map/ppermute | solution.py:31
  115.5 1.9 %convolution_convert_fusion.r_ref = bf16[512,640]{1,0:T(8,128)(2,1)S(1)} fusion(bf16[512,640]{1,0:T(8,128)(2,1)} %collective-permute-done.6, bf16[640,640]{1,0:T(8,128)(2,1)S(1)} %fusion.perm_ref), kind=kOutput, calls=%fused_computation.2 | convolution fusion | flops 419758080 | bytes 2129920 | tf_op jit(solution)/shard_map/dot_general | solution.py:194
  117.4 0.0 copy-start.3
  117.4 1.9 %collective-permute-start.8 = (bf16[512,640]{1,0:T(8,128)(2,1)S(1)}, bf16[512,640]{1,0:T(8,128)(2,1)}, u32[]{:S(2)}, u32[]{:S(2)}) collective-permute-start(bf16[512,640]{1,0:T(8,128)(2,1)S(1)} %convolution_convert_fusion.r_ref), channel_id=1, source_target_pairs={{0,1},{1,2},{2,3},{3,0},{8,9},{9,10},{10,11},{11,8},{16,17},{17,18... | collective-permute-start | bytes 1966088 | tf_op jit(solution)/shard_map/ppermute | solution.py:31
  119.3 1.6 convolution_convert_fusion.2.s_ref
  120.9 2.1 %collective-permute-start.9 = (bf16[128,640]{1,0:T(8,128)(2,1)S(1)}, bf16[128,640]{1,0:T(8,128)(2,1)S(1)}, u32[]{:S(2)}, u32[]{:S(2)}) collective-permute-start(bf16[128,640]{1,0:T(8,128)(2,1)S(1)} %slice.19), channel_id=1, source_target_pairs={{0,2},{1,3},{2,0},{3,1},{8,10},{9,11},{10,8},{11,9},{16,18},{17,19... | collective-permute-start | bytes 491528 | tf_op jit(solution)/shard_map/ppermute | solution.py:31
  123.0 1.6 convolution_convert_fusion.1.a_ref
  124.6 0.0 copy-done
  124.6 0.0 copy-done.3
  124.6 1.0 convolution_convert_fusion.3.ts_ref
  125.6 13.9 %collective-permute-done.9.tr_ref = bf16[128,640]{1,0:T(8,128)(2,1)S(1)} collective-permute-done((bf16[128,640]{1,0:T(8,128)(2,1)S(1)}, bf16[128,640]{1,0:T(8,128)(2,1)S(1)}, u32[]{:S(2)}, u32[]{:S(2)}) %collective-permute-start.9) | collective-permute-done | bytes 163872 | tf_op jit(solution)/shard_map/ppermute | solution.py:31
  139.5 0.0 copy-start.4
  139.5 7.9 %collective-permute-done.8.b_ref = bf16[512,640]{1,0:T(8,128)(2,1)} collective-permute-done((bf16[512,640]{1,0:T(8,128)(2,1)S(1)}, bf16[512,640]{1,0:T(8,128)(2,1)}, u32[]{:S(2)}, u32[]{:S(2)}) %collective-permute-start.8) | collective-permute-done | bytes 655392 | tf_op jit(solution)/shard_map/ppermute | solution.py:31
  147.4 0.0 all-gather.3.cloned.1.call-done
  147.4 0.0 copy-done.4
  147.4 26.7 %shard_map.64 = bf16[512,640]{1,0:T(8,128)(2,1)} custom-call(s32[5]{0:T(128)} %stack.39.where, bf16[512,640]{1,0:T(8,128)(2,1)} %convolution_convert_fusion.2.s_ref, bf16[512,640]{1,0:T(8,128)(2,1)} %convolution_convert_fusion.1.a_ref, bf16[512,640]{1,0:T(8,128)(2,1)} %copy-done.3, bf16[512,640]{1,0:T(8,128)(2,1)} %collective-permute-done.8.b_ref, ...), custom_call_target="tpu_custom_call" | custom-call | flops 15000000512 | bytes 16000000 | tf_op jit(solution)/shard_map/pallas_call | solution.py:139
  (10 shorter events, 0.1 us)
Async XLA Ops:
  6.5 29.0 %copy-start.1 = (bf16[512,640]{1,0:T(8,128)(2,1)S(1)}, bf16[512,640]{1,0:T(8,128)(2,1)}, u32[]{:S(2)}) copy-start(bf16[512,640]{1,0:T(8,128)(2,1)} %param.6) | copy-start | bytes 1966084
  6.5 140.8 %all-gather.3.cloned.1.call-start = ((), (), s32[]{:S(2)}) async-start(), calls=%async_computation | async-start | bytes 13516800 | tf_op jit(solution)/shard_map/all_gather | solution.py:186
  7.5 9.3 %collective-permute-start.1 = (bf16[40,640]{1,0:T(8,128)(2,1)S(1)}, bf16[40,640]{1,0:T(8,128)(2,1)S(1)}, u32[]{:S(2)}, u32[]{:S(2)}) collective-permute-start(bf16[40,640]{1,0:T(8,128)(2,1)S(1)} %bitcast_select_fusion), channel_id=1, source_target_pairs={{0,452},{1,453},{2,454},{3,455},{8,460},{9,461},{10,462},{11,463},... | collective-permute-start | bytes 153608 | tf_op jit(solution)/shard_map/ppermute | solution.py:31
  9.4 14.9 %collective-permute-start = (bf16[40,640]{1,0:T(8,128)(2,1)S(1)}, bf16[40,640]{1,0:T(8,128)(2,1)S(1)}, u32[]{:S(2)}, u32[]{:S(2)}) collective-permute-start(bf16[40,640]{1,0:T(8,128)(2,1)S(1)} %bitcast_select_fusion), channel_id=1, source_target_pairs={{0,64},{1,65},{2,66},{3,67},{8,72},{9,73},{10,74},{11,75},{16,80},... | collective-permute-start | bytes 153608 | tf_op jit(solution)/shard_map/ppermute | solution.py:31
  13.0 21.8 %collective-permute-start.4 = (bf16[512,640]{1,0:T(8,128)(2,1)}, bf16[512,640]{1,0:T(8,128)(2,1)S(1)}, u32[]{:S(2)}, u32[]{:S(2)}) collective-permute-start(bf16[512,640]{1,0:T(8,128)(2,1)} %param.6), channel_id=1, source_target_pairs={{4,12},{5,13},{6,14},{7,15},{12,20},{13,21},{14,22},{15,23},{20,28... | collective-permute-start | bytes 1966088 | tf_op jit(solution)/shard_map/ppermute | solution.py:170
  13.7 21.1 %collective-permute-start.5 = (bf16[512,640]{1,0:T(8,128)(2,1)}, bf16[512,640]{1,0:T(8,128)(2,1)S(1)}, u32[]{:S(2)}, u32[]{:S(2)}) collective-permute-start(bf16[512,640]{1,0:T(8,128)(2,1)} %param.6), channel_id=1, source_target_pairs={{0,1},{1,2},{2,3},{3,8},{4,5},{5,6},{6,7},{7,12},{8,9},{9,10},{10,... | collective-permute-start | bytes 1966088 | tf_op jit(solution)/shard_map/ppermute | solution.py:36
  16.8 17.9 %collective-permute-start.3 = (bf16[80,640]{1,0:T(8,128)(2,1)S(1)}, bf16[80,640]{1,0:T(8,128)(2,1)S(1)}, u32[]{:S(2)}, u32[]{:S(2)}) collective-permute-start(bf16[80,640]{1,0:T(8,128)(2,1)S(1)} %pad_maximum_fusion.1), channel_id=1, source_target_pairs={{0,192},{1,193},{2,194},{3,195},{8,200},{9,201},{10,202},{11,203},... | collective-permute-start | bytes 307208 | tf_op jit(solution)/shard_map/ppermute | solution.py:31
  24.3 10.3 %collective-permute-start.2 = (bf16[120,640]{1,0:T(8,128)(2,1)S(1)}, bf16[120,640]{1,0:T(8,128)(2,1)S(1)}, u32[]{:S(2)}, u32[]{:S(2)}) collective-permute-start(bf16[120,640]{1,0:T(8,128)(2,1)S(1)} %pad_maximum_fusion), channel_id=1, source_target_pairs={{0,324},{1,325},{2,326},{3,327},{8,332},{9,333},{10,334},{11,335},... | collective-permute-start | bytes 460808 | tf_op jit(solution)/shard_map/ppermute | solution.py:31
  34.7 0.8 copy-start.2
  35.6 79.9 %collective-permute-start.6 = (bf16[512,640]{1,0:T(8,128)(2,1)S(1)}, bf16[512,640]{1,0:T(8,128)(2,1)}, u32[]{:S(2)}, u32[]{:S(2)}) collective-permute-start(bf16[512,640]{1,0:T(8,128)(2,1)S(1)} %broadcast_select_fusion), channel_id=1, source_target_pairs={{0,4},{1,5},{2,6},{3,7},{8,12},{9,13},{10,14},{11,15},{16,20},{17,... | collective-permute-start | bytes 1966088 | tf_op jit(solution)/shard_map/ppermute | solution.py:31
  63.5 13.8 %collective-permute-start.7 = (bf16[128,640]{1,0:T(8,128)(2,1)S(1)}, bf16[128,640]{1,0:T(8,128)(2,1)S(1)}, u32[]{:S(2)}, u32[]{:S(2)}) collective-permute-start(bf16[128,640]{1,0:T(8,128)(2,1)S(1)} %slice.8), channel_id=1, source_target_pairs={{0,2},{1,3},{2,8},{3,9},{4,6},{5,7},{6,12},{7,13},{8,10},{9,11},{1... | collective-permute-start | bytes 491528 | tf_op jit(solution)/shard_map/ppermute | solution.py:36
  65.7 58.9 %copy-start = (bf16[640,640]{1,0:T(8,128)(2,1)}, bf16[640,640]{1,0:T(8,128)(2,1)S(1)}, u32[]{:S(2)}) copy-start(bf16[640,640]{1,0:T(8,128)(2,1)S(1)} %fusion.perm_ref) | copy-start | bytes 2457604
  117.4 7.2 %copy-start.3 = (bf16[512,640]{1,0:T(8,128)(2,1)}, bf16[512,640]{1,0:T(8,128)(2,1)S(1)}, u32[]{:S(2)}) copy-start(bf16[512,640]{1,0:T(8,128)(2,1)S(1)} %convolution_convert_fusion.r_ref) | copy-start | bytes 1966084
  117.4 30.0 %collective-permute-start.8 = (bf16[512,640]{1,0:T(8,128)(2,1)S(1)}, bf16[512,640]{1,0:T(8,128)(2,1)}, u32[]{:S(2)}, u32[]{:S(2)}) collective-permute-start(bf16[512,640]{1,0:T(8,128)(2,1)S(1)} %convolution_convert_fusion.r_ref), channel_id=1, source_target_pairs={{0,1},{1,2},{2,3},{3,0},{8,9},{9,10},{10,11},{11,8},{16,17},{17,18... | collective-permute-start | bytes 1966088 | tf_op jit(solution)/shard_map/ppermute | solution.py:31
  120.9 18.6 %collective-permute-start.9 = (bf16[128,640]{1,0:T(8,128)(2,1)S(1)}, bf16[128,640]{1,0:T(8,128)(2,1)S(1)}, u32[]{:S(2)}, u32[]{:S(2)}) collective-permute-start(bf16[128,640]{1,0:T(8,128)(2,1)S(1)} %slice.19), channel_id=1, source_target_pairs={{0,2},{1,3},{2,0},{3,1},{8,10},{9,11},{10,8},{11,9},{16,18},{17,19... | collective-permute-start | bytes 491528 | tf_op jit(solution)/shard_map/ppermute | solution.py:31
  139.5 7.9 %copy-start.4 = (bf16[128,640]{1,0:T(8,128)(2,1)}, bf16[128,640]{1,0:T(8,128)(2,1)S(1)}, u32[]{:S(2)}) copy-start(bf16[128,640]{1,0:T(8,128)(2,1)S(1)} %collective-permute-done.9.tr_ref) | copy-start | bytes 491524
Sparse Core Ops, SparseCore 0:
  35.6 107.0 all-gather.2

commit v5 on v4

--- a/solution.py
+++ b/solution.py
@@ -188,17 +188,17 @@
         jnp.where(zh == 1, stepped, own), lambda z, c, yy, xx: (z + 8, c, yy, xx)
     )
     own_tail = shifted(own[BLOCK - TAIL :], lambda b: b + 2 if b % 4 < 2 else b + 6)
-    far, beside, own_tail, perm = lax.optimization_barrier((far, beside, own_tail, perm))
-
     def reordered(rows):
         return jnp.dot(rows, perm, preferred_element_type=jnp.float32).astype(jnp.bfloat16)
+
+    ready = reordered(own), reordered(beside)
+    far, ready, own_tail, perm = lax.optimization_barrier((far, ready, own_tail, perm))
 
     far = reordered(far)
     far_beside = permuted(far, lambda z, c, yy, xx: (z, c, yy, xx + 1))
     far_tail = permuted(far[BLOCK - TAIL :], lambda z, c, yy, xx: (z, c, yy, xx + 2))
 
-    own, beside, own_tail = reordered(own), reordered(beside), reordered(own_tail)
-    rows_in = (own, beside, far, far_beside, own_tail, far_tail)
+    rows_in = (*ready, far, far_beside, reordered(own_tail), far_tail)
     return block_output(where, rows_in, perm, conv_bias, weights)
 
 

time: 181 us -> 181 us (level)
    ppermute x2, waiting for transfers between devices: 11.6 us -> 8.81 us  [shifted(): return lax.ppermute(value, AXES, [(a, b) for a, b in pairs if b < DEVICES])]
    ppermute x7, waiting for transfers between devices: 62.4 us -> 65 us  [permuted(): return lax.ppermute(value, AXES, pairs)]
  transfers between devices with their start and end apart: 11 -> 11, of which waited for: 5 -> 5; matrix products, arithmetic and copies ran while one was open for 4% -> 3% of each run, Pallas kernels for 0% -> 0%
where the time goes in v5:
time: 181 us
  waiting for transfers between devices  73.8 us (41%)
  starting transfers between devices  57.7 us (32%)
  Pallas kernels  26.7 us (15%)
  between operations  13.7 us (8%)
  matrix products  4.95 us (3%)
  local copies, waits for them, and re-layouts  2.29 us (1%)
    ppermute x7, waiting for transfers between devices, permuted(): return lax.ppermute(value, AXES, pairs)  65 us
    ppermute x7, starting transfers between devices, permuted(): return lax.ppermute(value, AXES, pairs)  52 us
    pallas_call x1, Pallas kernels, block_output(): pl.pallas_call(kernel, out_shape=jax.ShapeDtypeStruct((BLOCK, D), jnp.bfl...  26.7 us
    ppermute x2, waiting for transfers between devices, shifted(): return lax.ppermute(value, AXES, [(a, b) for a, b in pairs if b < DEVICES])  8.81 us
    ppermute x2, starting transfers between devices, shifted(): return lax.ppermute(value, AXES, [(a, b) for a, b in pairs if b < DEVICES])  5.04 us
    dot_general x4, matrix products, reordered(): jnp.dot(rows, perm, preferred_element_type=jnp.float32).astype(jnp.bfloat16)  4.95 us
  transfers between devices with their start and end apart: 11, of which 5 were waited for; matrix products, arithmetic and copies ran while one was open for 3% of the time, Pallas kernels for 0%

profile of v5, /device:TPU:33, one launch (start us, length us, event | category | flops | bytes accessed | tf_op | source)
XLA Modules:
  0.0 180.6 jit_solution(15541151119541846279)
XLA Ops:
  6.5 0.0 copy-start.1
  6.5 0.0 all-gather.3.cloned.1.call-start
  6.5 0.9 bitcast_select_fusion
  7.5 1.9 %collective-permute-start.1 = (bf16[40,640]{1,0:T(8,128)(2,1)S(1)}, bf16[40,640]{1,0:T(8,128)(2,1)S(1)}, u32[]{:S(2)}, u32[]{:S(2)}) collective-permute-start(bf16[40,640]{1,0:T(8,128)(2,1)S(1)} %bitcast_select_fusion), channel_id=1, source_target_pairs={{0,452},{1,453},{2,454},{3,455},{8,460},{9,461},{10,462},{11,463},... | collective-permute-start | bytes 153608 | tf_op jit(solution)/shard_map/ppermute | solution.py:31
  9.4 3.5 %collective-permute-start = (bf16[40,640]{1,0:T(8,128)(2,1)S(1)}, bf16[40,640]{1,0:T(8,128)(2,1)S(1)}, u32[]{:S(2)}, u32[]{:S(2)}) collective-permute-start(bf16[40,640]{1,0:T(8,128)(2,1)S(1)} %bitcast_select_fusion), channel_id=1, source_target_pairs={{0,64},{1,65},{2,66},{3,67},{8,72},{9,73},{10,74},{11,75},{16,80},... | collective-permute-start | bytes 153608 | tf_op jit(solution)/shard_map/ppermute | solution.py:31
  13.0 0.7 collective-permute-start.4
  13.7 3.1 %collective-permute-start.5 = (bf16[512,640]{1,0:T(8,128)(2,1)}, bf16[512,640]{1,0:T(8,128)(2,1)S(1)}, u32[]{:S(2)}, u32[]{:S(2)}) collective-permute-start(bf16[512,640]{1,0:T(8,128)(2,1)} %param.6), channel_id=1, source_target_pairs={{0,1},{1,2},{2,3},{3,8},{4,5},{5,6},{6,7},{7,12},{8,9},{9,10},{10,... | collective-permute-start | bytes 1966088 | tf_op jit(solution)/shard_map/ppermute | solution.py:36
  16.8 0.0 collective-permute-done.1
  16.8 7.5 %collective-permute-start.3 = (bf16[80,640]{1,0:T(8,128)(2,1)S(1)}, bf16[80,640]{1,0:T(8,128)(2,1)S(1)}, u32[]{:S(2)}, u32[]{:S(2)}) collective-permute-start(bf16[80,640]{1,0:T(8,128)(2,1)S(1)} %pad_maximum_fusion.1), channel_id=1, source_target_pairs={{0,192},{1,193},{2,194},{3,195},{8,200},{9,201},{10,202},{11,203},... | collective-permute-start | bytes 307208 | tf_op jit(solution)/shard_map/ppermute | solution.py:31
  24.3 0.0 collective-permute-done
  24.3 7.9 %collective-permute-start.2 = (bf16[120,640]{1,0:T(8,128)(2,1)S(1)}, bf16[120,640]{1,0:T(8,128)(2,1)S(1)}, u32[]{:S(2)}, u32[]{:S(2)}) collective-permute-start(bf16[120,640]{1,0:T(8,128)(2,1)S(1)} %pad_maximum_fusion), channel_id=1, source_target_pairs={{0,324},{1,325},{2,326},{3,327},{8,332},{9,333},{10,334},{11,335},... | collective-permute-start | bytes 460808 | tf_op jit(solution)/shard_map/ppermute | solution.py:31
  32.3 2.4 %collective-permute-done.2 = bf16[120,640]{1,0:T(8,128)(2,1)S(1)} collective-permute-done((bf16[120,640]{1,0:T(8,128)(2,1)S(1)}, bf16[120,640]{1,0:T(8,128)(2,1)S(1)}, u32[]{:S(2)}, u32[]{:S(2)}) %collective-permute-start.2) | collective-permute-done | bytes 153632 | tf_op jit(solution)/shard_map/ppermute | solution.py:31
  34.7 0.0 collective-permute-done.3
  34.7 0.0 copy-start.2
  34.8 0.0 collective-permute-done.4
  34.8 0.0 collective-permute-done.5
  34.8 0.7 copy-done.2
  35.5 0.0 all-gather.3.cloned.1.call-update
  35.5 0.1 compare_reduce_fusion
  35.6 0.1 fusion.18
  35.7 0.0 copy-done.1
  35.7 0.1 broadcast_select_fusion
  35.8 27.1 %collective-permute-start.6 = (bf16[512,640]{1,0:T(8,128)(2,1)S(1)}, bf16[512,640]{1,0:T(8,128)(2,1)S(1)}, u32[]{:S(2)}, u32[]{:S(2)}) collective-permute-start(bf16[512,640]{1,0:T(8,128)(2,1)S(1)} %broadcast_select_fusion), channel_id=1, source_target_pairs={{0,4},{1,5},{2,6},{3,7},{8,12},{9,13},{10,14},{11,15},{16,20},{17,... | collective-permute-start | bytes 1966088 | tf_op jit(solution)/shard_map/ppermute | solution.py:31
  62.9 0.2 fusion.perm_ref
  63.2 0.0 copy-start
  63.2 1.9 %collective-permute-start.7 = (bf16[128,640]{1,0:T(8,128)(2,1)S(1)}, bf16[128,640]{1,0:T(8,128)(2,1)S(1)}, u32[]{:S(2)}, u32[]{:S(2)}) collective-permute-start(bf16[128,640]{1,0:T(8,128)(2,1)S(1)} %slice.8), channel_id=1, source_target_pairs={{0,2},{1,3},{2,8},{3,9},{4,6},{5,7},{6,12},{7,13},{8,10},{9,11},{1... | collective-permute-start | bytes 491528 | tf_op jit(solution)/shard_map/ppermute | solution.py:36
  65.1 1.6 fusion.3.s_ref
  66.7 1.6 fusion.4.a_ref
  68.4 8.8 %collective-permute-done.7 = bf16[128,640]{1,0:T(8,128)(2,1)S(1)} collective-permute-done((bf16[128,640]{1,0:T(8,128)(2,1)S(1)}, bf16[128,640]{1,0:T(8,128)(2,1)S(1)}, u32[]{:S(2)}, u32[]{:S(2)}) %collective-permute-start.7) | collective-permute-done | bytes 163872 | tf_op jit(solution)/shard_map/ppermute | solution.py:36
  77.2 38.3 %collective-permute-done.6 = bf16[512,640]{1,0:T(8,128)(2,1)S(1)} collective-permute-done((bf16[512,640]{1,0:T(8,128)(2,1)S(1)}, bf16[512,640]{1,0:T(8,128)(2,1)S(1)}, u32[]{:S(2)}, u32[]{:S(2)}) %collective-permute-start.6) | collective-permute-done | bytes 655392 | tf_op jit(solution)/shard_map/ppermute | solution.py:31
  115.5 0.7 convolution_convert_fusion.r_ref
  116.3 0.0 copy-start.3
  116.3 1.9 %collective-permute-start.8 = (bf16[512,640]{1,0:T(8,128)(2,1)S(1)}, bf16[512,640]{1,0:T(8,128)(2,1)S(1)}, u32[]{:S(2)}, u32[]{:S(2)}) collective-permute-start(bf16[512,640]{1,0:T(8,128)(2,1)S(1)} %convolution_convert_fusion.r_ref), channel_id=1, source_target_pairs={{0,1},{1,2},{2,3},{3,0},{8,9},{9,10},{10,11},{11,8},{16,17},{17,18... | collective-permute-start | bytes 1966088 | tf_op jit(solution)/shard_map/ppermute | solution.py:31
  118.2 0.6 stack.39.where
  118.8 2.1 %collective-permute-start.9 = (bf16[128,640]{1,0:T(8,128)(2,1)S(1)}, bf16[128,640]{1,0:T(8,128)(2,1)S(1)}, u32[]{:S(2)}, u32[]{:S(2)}) collective-permute-start(bf16[128,640]{1,0:T(8,128)(2,1)S(1)} %slice.19), channel_id=1, source_target_pairs={{0,2},{1,3},{2,0},{3,1},{8,10},{9,11},{10,8},{11,9},{16,18},{17,19... | collective-permute-start | bytes 491528 | tf_op jit(solution)/shard_map/ppermute | solution.py:31
  121.0 0.0 copy-done
  121.0 1.0 convolution_convert_fusion.1.ts_ref
  121.9 17.0 %collective-permute-done.9.tr_ref = bf16[128,640]{1,0:T(8,128)(2,1)S(1)} collective-permute-done((bf16[128,640]{1,0:T(8,128)(2,1)S(1)}, bf16[128,640]{1,0:T(8,128)(2,1)S(1)}, u32[]{:S(2)}, u32[]{:S(2)}) %collective-permute-start.9) | collective-permute-done | bytes 163872 | tf_op jit(solution)/shard_map/ppermute | solution.py:31
  138.9 0.0 copy-start.5
  138.9 7.2 %collective-permute-done.8.b_ref = bf16[512,640]{1,0:T(8,128)(2,1)S(1)} collective-permute-done((bf16[512,640]{1,0:T(8,128)(2,1)S(1)}, bf16[512,640]{1,0:T(8,128)(2,1)S(1)}, u32[]{:S(2)}, u32[]{:S(2)}) %collective-permute-start.8) | collective-permute-done | bytes 655392 | tf_op jit(solution)/shard_map/ppermute | solution.py:31
  146.2 0.0 copy-start.4
  146.2 0.0 all-gather.3.cloned.1.call-done
  146.2 0.0 copy-done.3
  146.2 0.0 copy-done.5
  146.2 0.8 copy-done.4
  147.0 26.7 %shard_map.64 = bf16[512,640]{1,0:T(8,128)(2,1)} custom-call(s32[5]{0:T(128)} %stack.39.where, bf16[512,640]{1,0:T(8,128)(2,1)} %fusion.3.s_ref, bf16[512,640]{1,0:T(8,128)(2,1)} %fusion.4.a_ref, bf16[512,640]{1,0:T(8,128)(2,1)} %copy-done.3, bf16[512,640]{1,0:T(8,128)(2,1)} %copy-done.4, bf16[128,640]{1,0:T(8,128)(2,1)} %convolution_convert_fusion.1.ts_ref, ...), custom_call_target="tpu_custom_call" | custom-call | flops 15000000512 | bytes 16000000 | tf_op jit(solution)/shard_map/pallas_call | solution.py:139
  (10 shorter events, 0.1 us)
Async XLA Ops:
  6.5 29.1 %copy-start.1 = (bf16[512,640]{1,0:T(8,128)(2,1)S(1)}, bf16[512,640]{1,0:T(8,128)(2,1)}, u32[]{:S(2)}) copy-start(bf16[512,640]{1,0:T(8,128)(2,1)} %param.6) | copy-start | bytes 1966084
  6.5 139.6 %all-gather.3.cloned.1.call-start = ((), (), s32[]{:S(2)}) async-start(), calls=%async_computation | async-start | bytes 13516800 | tf_op jit(solution)/shard_map/all_gather | solution.py:186
  7.5 9.3 %collective-permute-start.1 = (bf16[40,640]{1,0:T(8,128)(2,1)S(1)}, bf16[40,640]{1,0:T(8,128)(2,1)S(1)}, u32[]{:S(2)}, u32[]{:S(2)}) collective-permute-start(bf16[40,640]{1,0:T(8,128)(2,1)S(1)} %bitcast_select_fusion), channel_id=1, source_target_pairs={{0,452},{1,453},{2,454},{3,455},{8,460},{9,461},{10,462},{11,463},... | collective-permute-start | bytes 153608 | tf_op jit(solution)/shard_map/ppermute | solution.py:31
  9.4 14.9 %collective-permute-start = (bf16[40,640]{1,0:T(8,128)(2,1)S(1)}, bf16[40,640]{1,0:T(8,128)(2,1)S(1)}, u32[]{:S(2)}, u32[]{:S(2)}) collective-permute-start(bf16[40,640]{1,0:T(8,128)(2,1)S(1)} %bitcast_select_fusion), channel_id=1, source_target_pairs={{0,64},{1,65},{2,66},{3,67},{8,72},{9,73},{10,74},{11,75},{16,80},... | collective-permute-start | bytes 153608 | tf_op jit(solution)/shard_map/ppermute | solution.py:31
  13.0 21.8 %collective-permute-start.4 = (bf16[512,640]{1,0:T(8,128)(2,1)}, bf16[512,640]{1,0:T(8,128)(2,1)S(1)}, u32[]{:S(2)}, u32[]{:S(2)}) collective-permute-start(bf16[512,640]{1,0:T(8,128)(2,1)} %param.6), channel_id=1, source_target_pairs={{4,12},{5,13},{6,14},{7,15},{12,20},{13,21},{14,22},{15,23},{20,28... | collective-permute-start | bytes 1966088 | tf_op jit(solution)/shard_map/ppermute | solution.py:170
  13.7 21.1 %collective-permute-start.5 = (bf16[512,640]{1,0:T(8,128)(2,1)}, bf16[512,640]{1,0:T(8,128)(2,1)S(1)}, u32[]{:S(2)}, u32[]{:S(2)}) collective-permute-start(bf16[512,640]{1,0:T(8,128)(2,1)} %param.6), channel_id=1, source_target_pairs={{0,1},{1,2},{2,3},{3,8},{4,5},{5,6},{6,7},{7,12},{8,9},{9,10},{10,... | collective-permute-start | bytes 1966088 | tf_op jit(solution)/shard_map/ppermute | solution.py:36
  16.8 17.9 %collective-permute-start.3 = (bf16[80,640]{1,0:T(8,128)(2,1)S(1)}, bf16[80,640]{1,0:T(8,128)(2,1)S(1)}, u32[]{:S(2)}, u32[]{:S(2)}) collective-permute-start(bf16[80,640]{1,0:T(8,128)(2,1)S(1)} %pad_maximum_fusion.1), channel_id=1, source_target_pairs={{0,192},{1,193},{2,194},{3,195},{8,200},{9,201},{10,202},{11,203},... | collective-permute-start | bytes 307208 | tf_op jit(solution)/shard_map/ppermute | solution.py:31
  24.3 10.3 %collective-permute-start.2 = (bf16[120,640]{1,0:T(8,128)(2,1)S(1)}, bf16[120,640]{1,0:T(8,128)(2,1)S(1)}, u32[]{:S(2)}, u32[]{:S(2)}) collective-permute-start(bf16[120,640]{1,0:T(8,128)(2,1)S(1)} %pad_maximum_fusion), channel_id=1, source_target_pairs={{0,324},{1,325},{2,326},{3,327},{8,332},{9,333},{10,334},{11,335},... | collective-permute-start | bytes 460808 | tf_op jit(solution)/shard_map/ppermute | solution.py:31
  34.7 0.8 copy-start.2
  35.8 79.7 %collective-permute-start.6 = (bf16[512,640]{1,0:T(8,128)(2,1)S(1)}, bf16[512,640]{1,0:T(8,128)(2,1)S(1)}, u32[]{:S(2)}, u32[]{:S(2)}) collective-permute-start(bf16[512,640]{1,0:T(8,128)(2,1)S(1)} %broadcast_select_fusion), channel_id=1, source_target_pairs={{0,4},{1,5},{2,6},{3,7},{8,12},{9,13},{10,14},{11,15},{16,20},{17,... | collective-permute-start | bytes 1966088 | tf_op jit(solution)/shard_map/ppermute | solution.py:31
  63.2 57.8 %copy-start = (bf16[640,640]{1,0:T(8,128)(2,1)}, bf16[640,640]{1,0:T(8,128)(2,1)S(1)}, u32[]{:S(2)}) copy-start(bf16[640,640]{1,0:T(8,128)(2,1)S(1)} %fusion.perm_ref) | copy-start | bytes 2457604
  63.2 14.0 %collective-permute-start.7 = (bf16[128,640]{1,0:T(8,128)(2,1)S(1)}, bf16[128,640]{1,0:T(8,128)(2,1)S(1)}, u32[]{:S(2)}, u32[]{:S(2)}) collective-permute-start(bf16[128,640]{1,0:T(8,128)(2,1)S(1)} %slice.8), channel_id=1, source_target_pairs={{0,2},{1,3},{2,8},{3,9},{4,6},{5,7},{6,12},{7,13},{8,10},{9,11},{1... | collective-permute-start | bytes 491528 | tf_op jit(solution)/shard_map/ppermute | solution.py:36
  116.3 29.9 %copy-start.3 = (bf16[512,640]{1,0:T(8,128)(2,1)}, bf16[512,640]{1,0:T(8,128)(2,1)S(1)}, u32[]{:S(2)}) copy-start(bf16[512,640]{1,0:T(8,128)(2,1)S(1)} %convolution_convert_fusion.r_ref) | copy-start | bytes 1966084
  116.3 29.9 %collective-permute-start.8 = (bf16[512,640]{1,0:T(8,128)(2,1)S(1)}, bf16[512,640]{1,0:T(8,128)(2,1)S(1)}, u32[]{:S(2)}, u32[]{:S(2)}) collective-permute-start(bf16[512,640]{1,0:T(8,128)(2,1)S(1)} %convolution_convert_fusion.r_ref), channel_id=1, source_target_pairs={{0,1},{1,2},{2,3},{3,0},{8,9},{9,10},{10,11},{11,8},{16,17},{17,18... | collective-permute-start | bytes 1966088 | tf_op jit(solution)/shard_map/ppermute | solution.py:31
  118.8 20.1 %collective-permute-start.9 = (bf16[128,640]{1,0:T(8,128)(2,1)S(1)}, bf16[128,640]{1,0:T(8,128)(2,1)S(1)}, u32[]{:S(2)}, u32[]{:S(2)}) collective-permute-start(bf16[128,640]{1,0:T(8,128)(2,1)S(1)} %slice.19), channel_id=1, source_target_pairs={{0,2},{1,3},{2,0},{3,1},{8,10},{9,11},{10,8},{11,9},{16,18},{17,19... | collective-permute-start | bytes 491528 | tf_op jit(solution)/shard_map/ppermute | solution.py:31
  138.9 7.2 %copy-start.5 = (bf16[128,640]{1,0:T(8,128)(2,1)}, bf16[128,640]{1,0:T(8,128)(2,1)S(1)}, u32[]{:S(2)}) copy-start(bf16[128,640]{1,0:T(8,128)(2,1)S(1)} %collective-permute-done.9.tr_ref) | copy-start | bytes 491524
  146.2 0.9 copy-start.4
Sparse Core Ops, SparseCore 0:
  35.6 106.1 all-gather.2
